TPU v7x, 32 devices: a whole 2x2x4 slice. The times are simulated.
32 devices in a mesh: dp: 4 (over y, core), fsdp: 8 (over z, x).
Axes of the slice: x: 2, y: 2, z: 4, core: 2. Of those that a mesh axis runs over, the one named last changes fastest.
Arguments:
- tokens: bfloat16 [32, 1024, 768], P(('dp', 'fsdp')), may hold values from -6 to 6
- lengths: int32 [32], P(('dp', 'fsdp')), may hold values from 128 to 1024, as said below
- cotangent: bfloat16 [32, 1024, 768], P(('dp', 'fsdp')), may hold values from -6 to 6
- query_weight: bfloat16 [768, 768], P(('dp', 'fsdp')), may hold values from -0.21875 to 0.21875
- query_bias: bfloat16 [768], P(('dp', 'fsdp')), may hold values from -1.75 to 1.75
- keyval_weight: bfloat16 [768, 128], P(('dp', 'fsdp')), may hold values from -0.21875 to 0.21875
- keyval_bias: bfloat16 [128], P(('dp', 'fsdp')), may hold values from -1.75 to 1.75
- out_weight: bfloat16 [768, 768], P(('dp', 'fsdp')), may hold values from -2.5 to 2.5
- out_bias: bfloat16 [768], P(('dp', 'fsdp')), may hold values from -1.75 to 1.75
- norm_attn_gain: bfloat16 [768], P(('dp', 'fsdp')), may hold values from 0.5 to 1.5
- norm_attn_bias: bfloat16 [768], P(('dp', 'fsdp')), may hold values from -1.75 to 1.75
- norm_mlp_gain: bfloat16 [768], P(('dp', 'fsdp')), may hold values from 0.5 to 1.5
- norm_mlp_bias: bfloat16 [768], P(('dp', 'fsdp')), may hold values from -1.75 to 1.75
- up_weight: bfloat16 [768, 3072], P(('dp', 'fsdp')), may hold values from -0.21875 to 0.21875
- up_bias: bfloat16 [3072], P(('dp', 'fsdp')), may hold values from -1.75 to 1.75
- down_weight: bfloat16 [3072, 768], P(('dp', 'fsdp')), may hold values from -0.109375 to 0.109375
- down_bias: bfloat16 [768], P(('dp', 'fsdp')), may hold values from -1.75 to 1.75
Outputs:
- layer_out: bfloat16 [32, 1024, 768], P(('dp', 'fsdp'))
- grad_tokens: float32 [32, 1024, 768], P(('dp', 'fsdp'))
- grad_query_weight: float32 [768, 768], P(('dp', 'fsdp'))
- grad_query_bias: float32 [768], P(('dp', 'fsdp'))
- grad_keyval_weight: float32 [768, 128], P(('dp', 'fsdp'))
- grad_keyval_bias: float32 [128], P(('dp', 'fsdp'))
- grad_out_weight: float32 [768, 768], P(('dp', 'fsdp'))
- grad_out_bias: float32 [768], P(('dp', 'fsdp'))
- grad_norm_attn_gain: float32 [768], P(('dp', 'fsdp'))
- grad_norm_attn_bias: float32 [768], P(('dp', 'fsdp'))
- grad_norm_mlp_gain: float32 [768], P(('dp', 'fsdp'))
- grad_norm_mlp_bias: float32 [768], P(('dp', 'fsdp'))
- grad_up_weight: float32 [768, 3072], P(('dp', 'fsdp'))
- grad_up_bias: float32 [3072], P(('dp', 'fsdp'))
- grad_down_weight: float32 [3072, 768], P(('dp', 'fsdp'))
- grad_down_bias: float32 [768], P(('dp', 'fsdp'))
Inputs may be any that keep to these rules, and one draw needn't show every extreme that they name: `lengths`: some sequence has length exactly 1024 and some exactly 128; most sequences are long, a few short.
All inputs are finite; a program needn't handle non-finite values.
Results may differ from a plain program's by a relative error of at most 0.011.
Values may be sent and summed in bfloat16 or wider, within the bound.
No kernel may reach another device: no remote copies, remote signals or barrier semaphores. Data moves between devices by JAX's collectives and lax.ppermute only.
A program may use at most 256 MiB of HBM per device.

v0:
```python
import jax
import jax.numpy as jnp
from jax import lax
from jax.sharding import PartitionSpec as P

ROT = 16


eps_norm = 1e-05
neg_big = -1e30
root_half = 0.7071067811865476
inv_root_tau = 0.3989422804014327


def layer_norm(token_rows, norm_gain, norm_shift):
    average = jnp.mean(token_rows, axis=-1, keepdims=True)
    centred = token_rows - average
    spread = jnp.mean(centred * centred, axis=-1, keepdims=True)
    scaled = lax.rsqrt(spread + eps_norm)
    normed = centred * scaled
    return (normed * norm_gain.astype(jnp.float32) + norm_shift.astype(jnp.float32), normed, scaled)


def norm_back(grad_rows, normed, scaled, norm_gain):
    grad_gain = jnp.sum(grad_rows * normed, axis=0)
    grad_shift = jnp.sum(grad_rows, axis=0)
    centred_grad = grad_rows * norm_gain.astype(jnp.float32)
    grad_input = scaled * (
        centred_grad
        - jnp.mean(centred_grad, axis=-1, keepdims=True)
        - normed * jnp.mean(centred_grad * normed, axis=-1, keepdims=True)
    )
    return (grad_input, grad_gain, grad_shift)


def rotary_tables(seq_len, rot_dims):
    half_rot = rot_dims // 2
    inverse_freq = 10000.0 ** (-(2.0 * jnp.arange(half_rot, dtype=jnp.float32)) / rot_dims)
    angles = jnp.arange(seq_len, dtype=jnp.float32)[:, None] * inverse_freq[None, :]
    return (jnp.cos(angles), jnp.sin(angles))


def rotate(values, cosine_table, sine_table):
    half_rot = cosine_table.shape[-1]
    half_one = values[..., :half_rot]
    half_two = values[..., half_rot : 2 * half_rot]
    return jnp.concatenate(
        [
            half_one * cosine_table - half_two * sine_table,
            half_two * cosine_table + half_one * sine_table,
            values[..., 2 * half_rot :],
        ],
        axis=-1,
    )


def rotate_back(grad_rows, cosine_table, sine_table):
    half_rot = cosine_table.shape[-1]
    half_one = grad_rows[..., :half_rot]
    half_two = grad_rows[..., half_rot : 2 * half_rot]
    return jnp.concatenate(
        [
            half_one * cosine_table + half_two * sine_table,
            half_two * cosine_table - half_one * sine_table,
            grad_rows[..., 2 * half_rot :],
        ],
        axis=-1,
    )


def block_scores(query_block, key_rot, block_start, length, score_scale):
    block_rows = query_block.shape[0]
    seq_len = key_rot.shape[0]
    scores = (
        jnp.einsum("qhd,kd->hqk", query_block, key_rot, preferred_element_type=jnp.float32)
        * score_scale
    )
    key_pos = jnp.arange(seq_len, dtype=jnp.int32)
    query_pos = block_start + jnp.arange(block_rows, dtype=jnp.int32)
    allowed = (key_pos[None, :] <= query_pos[:, None]) & (key_pos[None, :] < length)
    return (jnp.where(allowed[None], scores, neg_big), allowed)


def attend_forward(seq_items):
    query_rot, key_rot, values, length = seq_items
    seq_len, head_count, head_dim = query_rot.shape
    block_rows = min(512, seq_len)
    block_count = seq_len // block_rows
    score_scale = head_dim ** (-0.5)

    def one_block(block_items):
        query_block, block_start = block_items
        scores, allowed = block_scores(query_block, key_rot, block_start, length, score_scale)
        row_max = jnp.max(scores, axis=-1, keepdims=True)
        exponent = jnp.exp(scores - row_max)
        totals = jnp.sum(exponent, axis=-1, keepdims=True)
        softmax_low = (exponent / totals).astype(jnp.bfloat16)
        mixed_heads = jnp.einsum(
            "hqk,kd->qhd", softmax_low, values, preferred_element_type=jnp.float32
        ).astype(jnp.bfloat16)
        return (mixed_heads, (row_max + jnp.log(totals))[..., 0])

    query_blocks = query_rot.reshape(block_count, block_rows, head_count, head_dim)
    starts = jnp.arange(block_count, dtype=jnp.int32) * block_rows
    mixed_heads, log_sums = lax.map(one_block, (query_blocks, starts))
    return (mixed_heads.reshape(seq_len, head_count, head_dim), log_sums)


def attend_backward(seq_items):
    query_rot, key_rot, values, length, log_sums, grad_mixed = seq_items
    seq_len, head_count, head_dim = query_rot.shape
    block_rows = min(512, seq_len)
    block_count = seq_len // block_rows
    score_scale = head_dim ** (-0.5)

    def one_block(running, block_items):
        grad_keys, grad_values = running
        query_block, grad_block, lse_block, block_start = block_items
        scores, allowed = block_scores(query_block, key_rot, block_start, length, score_scale)
        softmax_full = jnp.where(allowed[None], jnp.exp(scores - lse_block[..., None]), 0.0)
        softmax_low = softmax_full.astype(jnp.bfloat16)
        grad_values = grad_values + jnp.einsum(
            "hqk,qhd->kd", softmax_low, grad_block, preferred_element_type=jnp.float32
        )
        grad_probs = jnp.einsum(
            "qhd,kd->hqk", grad_block, values, preferred_element_type=jnp.float32
        )
        row_inner = jnp.sum(softmax_full * grad_probs, axis=-1, keepdims=True)
        grad_scores = (softmax_full * (grad_probs - row_inner)).astype(jnp.bfloat16)
        grad_query = (
            jnp.einsum("hqk,kd->qhd", grad_scores, key_rot, preferred_element_type=jnp.float32)
            * score_scale
        )
        grad_keys = (
            grad_keys
            + jnp.einsum(
                "hqk,qhd->kd", grad_scores, query_block, preferred_element_type=jnp.float32
            )
            * score_scale
        )
        return ((grad_keys, grad_values), grad_query)

    query_blocks = query_rot.reshape(block_count, block_rows, head_count, head_dim)
    grad_blocks = grad_mixed.reshape(block_count, block_rows, head_count, head_dim)
    starts = jnp.arange(block_count, dtype=jnp.int32) * block_rows
    zero_rows = jnp.zeros((seq_len, head_dim), jnp.float32)
    (grad_keys, grad_values), grad_query = lax.scan(
        one_block, (zero_rows, zero_rows), (query_blocks, grad_blocks, log_sums, starts)
    )
    return (grad_query.reshape(seq_len, head_count, head_dim), grad_keys, grad_values)


def collect(
    query_weight,
    query_bias,
    keyval_weight,
    keyval_bias,
    out_weight,
    out_bias,
    attn_gain,
    attn_shift,
    mlp_gain,
    mlp_shift,
    up_weight,
    up_bias,
    down_weight,
    down_bias,
):
    return (
        lax.all_gather(query_weight, ("dp", "fsdp"), axis=0, tiled=True),
        lax.all_gather(query_bias, ("dp", "fsdp"), axis=0, tiled=True),
        lax.all_gather(keyval_weight, ("dp", "fsdp"), axis=0, tiled=True),
        lax.all_gather(keyval_bias, ("dp", "fsdp"), axis=0, tiled=True),
        lax.all_gather(out_weight, ("dp", "fsdp"), axis=0, tiled=True),
        lax.all_gather(out_bias, ("dp", "fsdp"), axis=0, tiled=True),
        lax.all_gather(attn_gain, ("dp", "fsdp"), axis=0, tiled=True),
        lax.all_gather(attn_shift, ("dp", "fsdp"), axis=0, tiled=True),
        lax.all_gather(mlp_gain, ("dp", "fsdp"), axis=0, tiled=True),
        lax.all_gather(mlp_shift, ("dp", "fsdp"), axis=0, tiled=True),
        lax.all_gather(up_weight, ("dp", "fsdp"), axis=0, tiled=True),
        lax.all_gather(up_bias, ("dp", "fsdp"), axis=0, tiled=True),
        lax.all_gather(down_weight, ("dp", "fsdp"), axis=0, tiled=True),
        lax.all_gather(down_bias, ("dp", "fsdp"), axis=0, tiled=True),
    )


def spread(
    query_weight,
    query_bias,
    keyval_weight,
    keyval_bias,
    out_weight,
    out_bias,
    attn_gain,
    attn_shift,
    mlp_gain,
    mlp_shift,
    up_weight,
    up_bias,
    down_weight,
    down_bias,
):
    return (
        lax.psum_scatter(query_weight, ("dp", "fsdp"), scatter_dimension=0, tiled=True),
        lax.psum_scatter(query_bias, ("dp", "fsdp"), scatter_dimension=0, tiled=True),
        lax.psum_scatter(keyval_weight, ("dp", "fsdp"), scatter_dimension=0, tiled=True),
        lax.psum_scatter(keyval_bias, ("dp", "fsdp"), scatter_dimension=0, tiled=True),
        lax.psum_scatter(out_weight, ("dp", "fsdp"), scatter_dimension=0, tiled=True),
        lax.psum_scatter(out_bias, ("dp", "fsdp"), scatter_dimension=0, tiled=True),
        lax.psum_scatter(attn_gain, ("dp", "fsdp"), scatter_dimension=0, tiled=True),
        lax.psum_scatter(attn_shift, ("dp", "fsdp"), scatter_dimension=0, tiled=True),
        lax.psum_scatter(mlp_gain, ("dp", "fsdp"), scatter_dimension=0, tiled=True),
        lax.psum_scatter(mlp_shift, ("dp", "fsdp"), scatter_dimension=0, tiled=True),
        lax.psum_scatter(up_weight, ("dp", "fsdp"), scatter_dimension=0, tiled=True),
        lax.psum_scatter(up_bias, ("dp", "fsdp"), scatter_dimension=0, tiled=True),
        lax.psum_scatter(down_weight, ("dp", "fsdp"), scatter_dimension=0, tiled=True),
        lax.psum_scatter(down_bias, ("dp", "fsdp"), scatter_dimension=0, tiled=True),
    )


def forward(tokens, lengths, params, cosine_table, sine_table):
    (
        query_weight,
        query_bias,
        keyval_weight,
        keyval_bias,
        out_weight,
        out_bias,
        attn_gain,
        attn_shift,
        mlp_gain,
        mlp_shift,
        up_weight,
        up_bias,
        down_weight,
        down_bias,
    ) = params
    seq_count, seq_len, model_width = tokens.shape
    head_dim = keyval_weight.shape[1] // 2
    head_count = model_width // head_dim
    token_rows = tokens.reshape(seq_count * seq_len, model_width).astype(jnp.float32)
    h_attn_full, normed_attn, scaled_attn = layer_norm(token_rows, attn_gain, attn_shift)
    h_attn = h_attn_full.astype(jnp.bfloat16)
    query_lin = jnp.dot(
        h_attn, query_weight, preferred_element_type=jnp.float32
    ) + query_bias.astype(jnp.float32)
    keyval_lin = jnp.dot(
        h_attn, keyval_weight, preferred_element_type=jnp.float32
    ) + keyval_bias.astype(jnp.float32)
    query_rot = rotate(
        query_lin.reshape(seq_count, seq_len, head_count, head_dim),
        cosine_table[:, None, :],
        sine_table[:, None, :],
    ).astype(jnp.bfloat16)
    key_rot = rotate(
        keyval_lin[:, :head_dim].reshape(seq_count, seq_len, head_dim), cosine_table, sine_table
    ).astype(jnp.bfloat16)
    values = keyval_lin[:, head_dim:].reshape(seq_count, seq_len, head_dim).astype(jnp.bfloat16)
    mixed_heads, log_sums = lax.map(attend_forward, (query_rot, key_rot, values, lengths))
    mixed_heads = mixed_heads.reshape(seq_count * seq_len, model_width)
    attn_out = jnp.dot(
        mixed_heads, out_weight, preferred_element_type=jnp.float32
    ) + out_bias.astype(jnp.float32)
    h_mlp_full, normed_mlp, scaled_mlp = layer_norm(token_rows, mlp_gain, mlp_shift)
    h_mlp = h_mlp_full.astype(jnp.bfloat16)
    up_lin = jnp.dot(h_mlp, up_weight, preferred_element_type=jnp.float32) + up_bias.astype(
        jnp.float32
    )
    act_low = jax.nn.gelu(up_lin, approximate=False).astype(jnp.bfloat16)
    mlp_out = jnp.dot(act_low, down_weight, preferred_element_type=jnp.float32) + down_bias.astype(
        jnp.float32
    )
    row_keep = (
        (jnp.arange(seq_len, dtype=jnp.int32)[None, :] < lengths[:, None])
        .astype(jnp.float32)
        .reshape(seq_count * seq_len, 1)
    )
    layer_out = (
        (token_rows + row_keep * (attn_out + mlp_out))
        .astype(jnp.bfloat16)
        .reshape(seq_count, seq_len, model_width)
    )
    kept_state = (
        row_keep,
        h_attn,
        normed_attn,
        scaled_attn,
        query_rot,
        key_rot,
        values,
        mixed_heads,
        log_sums,
        h_mlp,
        normed_mlp,
        scaled_mlp,
        up_lin,
        act_low,
    )
    return (layer_out, kept_state)


def backward(cotangent, lengths, params, kept_state, cosine_table, sine_table):
    (
        query_weight,
        query_bias,
        keyval_weight,
        keyval_bias,
        out_weight,
        out_bias,
        attn_gain,
        attn_shift,
        mlp_gain,
        mlp_shift,
        up_weight,
        up_bias,
        down_weight,
        down_bias,
    ) = params
    (
        row_keep,
        h_attn,
        normed_attn,
        scaled_attn,
        query_rot,
        key_rot,
        values,
        mixed_heads,
        log_sums,
        h_mlp,
        normed_mlp,
        scaled_mlp,
        up_lin,
        act_low,
    ) = kept_state
    seq_count, seq_len, model_width = cotangent.shape
    head_dim = keyval_weight.shape[1] // 2
    head_count = model_width // head_dim
    grad_rows = cotangent.reshape(seq_count * seq_len, model_width).astype(jnp.float32)
    grad_masked = (grad_rows * row_keep).astype(jnp.bfloat16)
    grad_out_weight = jnp.einsum(
        "nd,ne->de", mixed_heads, grad_masked, preferred_element_type=jnp.float32
    )
    grad_down_weight = jnp.einsum(
        "nf,ne->fe", act_low, grad_masked, preferred_element_type=jnp.float32
    )
    grad_branch_bias = jnp.sum(grad_masked.astype(jnp.float32), axis=0)
    grad_mixed = jnp.einsum(
        "ne,de->nd", grad_masked, out_weight, preferred_element_type=jnp.float32
    ).astype(jnp.bfloat16)
    grad_act = jnp.einsum("ne,fe->nf", grad_masked, down_weight, preferred_element_type=jnp.float32)
    normal_cdf = 0.5 * (1.0 + lax.erf(up_lin * root_half))
    normal_pdf = jnp.exp(-0.5 * up_lin * up_lin) * inv_root_tau
    grad_up = (grad_act * (normal_cdf + up_lin * normal_pdf)).astype(jnp.bfloat16)
    grad_up_weight = jnp.einsum("nd,nf->df", h_mlp, grad_up, preferred_element_type=jnp.float32)
    grad_up_bias = jnp.sum(grad_up.astype(jnp.float32), axis=0)
    grad_h_mlp = jnp.einsum("nf,df->nd", grad_up, up_weight, preferred_element_type=jnp.float32)
    grad_in_mlp, grad_mlp_gain, grad_mlp_shift = norm_back(
        grad_h_mlp, normed_mlp, scaled_mlp, mlp_gain
    )
    grad_mixed_heads = grad_mixed.reshape(seq_count, seq_len, head_count, head_dim)
    grad_query_rot, grad_key_rot, grad_values = lax.map(
        attend_backward, (query_rot, key_rot, values, lengths, log_sums, grad_mixed_heads)
    )
    grad_query_lin = (
        rotate_back(grad_query_rot, cosine_table[:, None, :], sine_table[:, None, :])
        .reshape(seq_count * seq_len, model_width)
        .astype(jnp.bfloat16)
    )
    grad_keyval_lin = (
        jnp.concatenate([rotate_back(grad_key_rot, cosine_table, sine_table), grad_values], axis=-1)
        .reshape(seq_count * seq_len, 2 * head_dim)
        .astype(jnp.bfloat16)
    )
    grad_query_weight = jnp.einsum(
        "nd,ne->de", h_attn, grad_query_lin, preferred_element_type=jnp.float32
    )
    grad_query_bias = jnp.sum(grad_query_lin.astype(jnp.float32), axis=0)
    grad_keyval_weight = jnp.einsum(
        "nd,ne->de", h_attn, grad_keyval_lin, preferred_element_type=jnp.float32
    )
    grad_keyval_bias = jnp.sum(grad_keyval_lin.astype(jnp.float32), axis=0)
    grad_h_attn = jnp.einsum(
        "ne,de->nd", grad_query_lin, query_weight, preferred_element_type=jnp.float32
    ) + jnp.einsum("ne,de->nd", grad_keyval_lin, keyval_weight, preferred_element_type=jnp.float32)
    grad_in_attn, grad_attn_gain, grad_attn_shift = norm_back(
        grad_h_attn, normed_attn, scaled_attn, attn_gain
    )
    grad_tokens = (grad_rows + grad_in_attn + grad_in_mlp).reshape(seq_count, seq_len, model_width)
    param_grads = (
        grad_query_weight,
        grad_query_bias,
        grad_keyval_weight,
        grad_keyval_bias,
        grad_out_weight,
        grad_branch_bias,
        grad_attn_gain,
        grad_attn_shift,
        grad_mlp_gain,
        grad_mlp_shift,
        grad_up_weight,
        grad_up_bias,
        grad_down_weight,
        grad_branch_bias,
    )
    return (grad_tokens, param_grads)


def body(
    tokens,
    lengths,
    cotangent,
    query_weight,
    query_bias,
    keyval_weight,
    keyval_bias,
    out_weight,
    out_bias,
    norm_attn_gain,
    norm_attn_bias,
    norm_mlp_gain,
    norm_mlp_bias,
    up_weight,
    up_bias,
    down_weight,
    down_bias,
):
    cosine_table, sine_table = rotary_tables(tokens.shape[1], ROT)
    params = collect(
        query_weight,
        query_bias,
        keyval_weight,
        keyval_bias,
        out_weight,
        out_bias,
        norm_attn_gain,
        norm_attn_bias,
        norm_mlp_gain,
        norm_mlp_bias,
        up_weight,
        up_bias,
        down_weight,
        down_bias,
    )
    layer_out, kept_state = forward(tokens, lengths, params, cosine_table, sine_table)
    params = collect(
        query_weight,
        query_bias,
        keyval_weight,
        keyval_bias,
        out_weight,
        out_bias,
        norm_attn_gain,
        norm_attn_bias,
        norm_mlp_gain,
        norm_mlp_bias,
        up_weight,
        up_bias,
        down_weight,
        down_bias,
    )
    kept_state = forward(tokens, lengths, params, cosine_table, sine_table)[1]
    grad_tokens, param_grads = backward(
        cotangent, lengths, params, kept_state, cosine_table, sine_table
    )
    summed = spread(*param_grads)
    return (layer_out, grad_tokens) + tuple(summed)


def solution(mesh):
    return jax.shard_map(
        body,
        mesh=mesh,
        in_specs=(
            P(("dp", "fsdp"), None, None),
            P(("dp", "fsdp")),
            P(("dp", "fsdp"), None, None),
            P(("dp", "fsdp"), None),
            P(("dp", "fsdp")),
            P(("dp", "fsdp"), None),
            P(("dp", "fsdp")),
            P(("dp", "fsdp"), None),
            P(("dp", "fsdp")),
            P(("dp", "fsdp")),
            P(("dp", "fsdp")),
            P(("dp", "fsdp")),
            P(("dp", "fsdp")),
            P(("dp", "fsdp"), None),
            P(("dp", "fsdp")),
            P(("dp", "fsdp"), None),
            P(("dp", "fsdp")),
        ),
        out_specs=(
            P(("dp", "fsdp"), None, None),
            P(("dp", "fsdp"), None, None),
            P(("dp", "fsdp"), None),
            P(("dp", "fsdp")),
            P(("dp", "fsdp"), None),
            P(("dp", "fsdp")),
            P(("dp", "fsdp"), None),
            P(("dp", "fsdp")),
            P(("dp", "fsdp")),
            P(("dp", "fsdp")),
            P(("dp", "fsdp")),
            P(("dp", "fsdp")),
            P(("dp", "fsdp"), None),
            P(("dp", "fsdp")),
            P(("dp", "fsdp"), None),
            P(("dp", "fsdp")),
        ),
        check_vma=False,
    )
```

profile of v0, /device:TPU:0, one launch (start us, length us, event | category | flops | bytes accessed | tf_op | source)
XLA Modules:
  0.0 1045.3 jit_solution(1348458671008902506)
XLA Ops:
  17.7 42.5 %all-reduce.19 = (bf16[768]{0:T(1024)(128)(2,1)}, bf16[768]{0:T(1024)(128)(2,1)}, bf16[3072]{0:T(1024)(128)(2,1)}, bf16[768]{0:T(1024)(128)(2,1)}, bf16[768]{0:T...) all-reduce(bf16[768]{0:T(1024)(128)(2,1)S(1)} %dynamic-update-slice, ...), channel_id=1, replica_groups=mesh['dp'=4,'fsdp'=8] {'dp','fsdp'}, use_global_device_ids=true, to_apply=%add.6 | all-reduce | flops 8576 | bytes 34304
  64.2 67.6 %all_gather.58 = bf16[768,128]{1,0:T(8,128)(2,1)S(1)} all-gather(bf16[24,128]{1,0:T(8,128)(2,1)S(1)} %copy-done.49), channel_id=1, replica_groups=mesh['dp'=4,'fsdp'=8] {'dp','fsdp'}, dimensions={0}, use_global_device_ids=true | all-gather | bytes 202752 | tf_op jit(solution)/shard_map/all_gather | solution.py:172
  146.4 73.9 %while.65 = (s32[]{:T(128)}, bf16[2,512,12,64]{1,3,2,0:T(8,128)(2,1)}, f32[2,12,512]{2,1,0:T(8,128)S(1)}, s32[2]{0:T(128)S(1)}, s32[]{:T(128)}, /*index=5*/bf16[...) while((s32[]{:T(128)}, ...), condition=%wide.region_9.10_spmd, body=%wide.region_6.9_spmd.sunk | while | flops 1687547392 | bytes 180320912 | solution.py:105
  148.7 10.5 %bitcast_reduce_fusion.3 = (f32[12,512]{1,0:T(8,128)S(1)}, f32[512,12,1024]{2,0,1:T(8,128)}) fusion(pred[512,1024]{1,0:T(8,128)(4,1)S(1)} %fusion.219, bf16[1024,64]{0,1:T(8,128)(2,1)S(1)} %get-tuple-element.658, bf16[2,512,12,64]{1,3,2,0:T(8,128)(2,1)S(1)} %get-tuple-element.657, s32[]{:T(128)} %get-tuple-element.643), kind=kOutput, calls=%fused_computation.27.clone.1 | convolution fusion | flops 824174592 | bytes 26632196 | tf_op jit(solution)/shard_map/while/body/eval_jaxpr/while/body/eval_jaxpr/qhd,kd->hqk/dot_general | solution.py:75
  159.2 12.3 %fusion.220 = f32[12,512]{1,0:T(8,128)S(1)} fusion(f32[512,12,1024]{2,0,1:T(8,128)} %get-tuple-element.595, f32[12,512]{1,0:T(8,128)S(1)} %get-tuple-element.596, pred[512,1024]{1,0:T(8,128)(4,1)S(1)} %fusion.219), kind=kLoop, calls=%fused_computation.31.clone.1 | loop fusion | flops 25159680 | bytes 25739264 | tf_op jit(solution)/shard_map/while/body/eval_jaxpr/while/body/eval_jaxpr/reduce_sum | solution.py:96
  185.9 10.5 %bitcast_reduce_fusion.3 = (f32[12,512]{1,0:T(8,128)S(1)}, f32[512,12,1024]{2,0,1:T(8,128)}) fusion(pred[512,1024]{1,0:T(8,128)(4,1)S(1)} %fusion.219, bf16[1024,64]{0,1:T(8,128)(2,1)S(1)} %get-tuple-element.658, bf16[2,512,12,64]{1,3,2,0:T(8,128)(2,1)S(1)} %get-tuple-element.657, s32[]{:T(128)} %get-tuple-element.643), kind=kOutput, calls=%fused_computation.27.clone.1 | convolution fusion | flops 824174592 | bytes 26632196 | tf_op jit(solution)/shard_map/while/body/eval_jaxpr/while/body/eval_jaxpr/qhd,kd->hqk/dot_general | solution.py:75
  196.4 12.4 %fusion.220 = f32[12,512]{1,0:T(8,128)S(1)} fusion(f32[512,12,1024]{2,0,1:T(8,128)} %get-tuple-element.595, f32[12,512]{1,0:T(8,128)S(1)} %get-tuple-element.596, pred[512,1024]{1,0:T(8,128)(4,1)S(1)} %fusion.219), kind=kLoop, calls=%fused_computation.31.clone.1 | loop fusion | flops 25159680 | bytes 25739264 | tf_op jit(solution)/shard_map/while/body/eval_jaxpr/while/body/eval_jaxpr/reduce_sum | solution.py:96
  231.8 207.6 %while.66 = (s32[]{:T(128)}, f32[1024,64]{0,1:T(8,128)S(1)}, f32[1024,64]{0,1:T(8,128)}, f32[2,512,12,64]{1,0,3,2:T(2,128)}, s32[2]{0:T(128)S(1)}, /*index=5*/s3...) while((s32[]{:T(128)}, f32[1024,64]{0,1:T(8,128)S(1)}, ...), condition=%wide.region_12.13_spmd.clone, body=%wide.region_10.12_spmd.clone.sunk | while | flops 4141542912 | bytes 267647888 | solution.py:147
  232.2 10.5 %fusion.230 = f32[512,12,1024]{2,0,1:T(8,128)} fusion(bf16[2,512,12,64]{1,3,2,0:T(8,128)(2,1)S(1)} %get-tuple-element.693, s32[]{:T(128)} %get-tuple-element.674, bf16[1024,64]{0,1:T(8,128)(2,1)S(1)} %get-tuple-element.694), kind=kOutput, calls=%fused_computation.71.clone.1 | convolution fusion | flops 805306368 | bytes 26083332 | tf_op jit(solution)/shard_map/while/body/eval_jaxpr/while/body/eval_jaxpr/qhd,kd->hqk/dot_general | solution.py:75
  245.8 18.7 %fusion.232 = (f32[12,512]{1,0:T(8,128)S(1)}, f32[512,12,1024]{2,0,1:T(8,128)}) fusion(f32[12,512]{1,0:T(8,128)S(1)} %dynamic-slice_bitcast_fusion.2, f32[512,12,1024]{2,0,1:T(8,128)} %fusion.230, pred[512,1024]{1,0:T(8,128)(4,1)S(1)} %fusion.231, bf16[1024,64]{0,1:T(8,128)(2,1)} %get-tuple-element.697, ...), kind=kOutput, calls=%fused_computation.51.clone.1 | convolution fusion | flops 843048960 | bytes 52355584 | tf_op jit(solution)/shard_map/while/body/eval_jaxpr/while/body/eval_jaxpr/qhd,kd->hqk/dot_general | solution.py:125
  264.5 17.1 %fusion.233 = bf16[12,512,1024]{2,1,0:T(8,128)(2,1)S(1)} fusion(f32[512,12,1024]{2,0,1:T(8,128)} %get-tuple-element.608, f32[12,512]{1,0:T(8,128)S(1)} %get-tuple-element.609, f32[12,512]{1,0:T(8,128)S(1)} %dynamic-slice_bitcast_fusion.2, f32[512,12,1024]{2,0,1:T(8,128)} %fusion.230, pred[512,1024]{1,0:T(8,128)(4,1)S(1)} %fusion.231), kind=kLoop, calls=%fused_computation.53.clone.1 | loop fusion | flops 44040192 | bytes 63488000 | tf_op jit(solution)/shard_map/while/body/eval_jaxpr/while/body/eval_jaxpr/convert_element_type | solution.py:129
  287.9 28.8 %dynamic_update_slice.42 = f32[2,512,12,64]{1,0,3,2:T(2,128)} dynamic-update-slice(f32[2,512,12,64]{1,0,3,2:T(2,128)} %get-tuple-element.677, f32[1,512,12,64]{1,0,3,2:T(1,128)S(1)} %copy.69, s32[]{:T(128)} %get-tuple-element.674, s32[]{:T(128)} %constant.82.clone.1..sunk, s32[]{:T(128)} %constant.82.clone.1..sunk, s32[]{:T(128)} %constant.82.clone.1..sunk) | dynamic-update-slice | bytes 3145732 | tf_op jit(solution)/shard_map/while/body/eval_jaxpr/while/body/jit(dynamic_update_index_in_dim)/dynamic_update_slice | solution.py:147
  323.8 11.4 %fusion.235 = f32[1024,64]{0,1:T(8,128)S(1)} fusion(f32[12,512]{1,0:T(8,128)S(1)} %copy-done.10, f32[512,12,1024]{2,0,1:T(8,128)} %fusion.230, pred[512,1024]{1,0:T(8,128)(4,1)S(1)} %copy-done.3, bf16[2,512,12,64]{1,3,2,0:T(8,128)(2,1)S(1)} %copy-done.13, s32[]{:T(128)} %get-tuple-element.674, f32[1024,64]{0,1:T(8,128)S(1)} %copy-done.18, ...), kind=kOutput, calls=%fused_computation.66.clone.1 | convolution fusion | flops 836894720 | bytes 27557892 | tf_op jit(solution)/shard_map/while/body/eval_jaxpr/while/body/eval_jaxpr/hqk,qhd->kd/dot_general | solution.py:122
  335.9 10.2 fusion.230
  349.2 18.6 %fusion.232 = (f32[12,512]{1,0:T(8,128)S(1)}, f32[512,12,1024]{2,0,1:T(8,128)}) fusion(f32[12,512]{1,0:T(8,128)S(1)} %dynamic-slice_bitcast_fusion.2, f32[512,12,1024]{2,0,1:T(8,128)} %fusion.230, pred[512,1024]{1,0:T(8,128)(4,1)S(1)} %fusion.231, bf16[1024,64]{0,1:T(8,128)(2,1)} %get-tuple-element.697, ...), kind=kOutput, calls=%fused_computation.51.clone.1 | convolution fusion | flops 843048960 | bytes 52355584 | tf_op jit(solution)/shard_map/while/body/eval_jaxpr/while/body/eval_jaxpr/qhd,kd->hqk/dot_general | solution.py:125
  367.8 17.1 %fusion.233 = bf16[12,512,1024]{2,1,0:T(8,128)(2,1)S(1)} fusion(f32[512,12,1024]{2,0,1:T(8,128)} %get-tuple-element.608, f32[12,512]{1,0:T(8,128)S(1)} %get-tuple-element.609, f32[12,512]{1,0:T(8,128)S(1)} %dynamic-slice_bitcast_fusion.2, f32[512,12,1024]{2,0,1:T(8,128)} %fusion.230, pred[512,1024]{1,0:T(8,128)(4,1)S(1)} %fusion.231), kind=kLoop, calls=%fused_computation.53.clone.1 | loop fusion | flops 44040192 | bytes 63488000 | tf_op jit(solution)/shard_map/while/body/eval_jaxpr/while/body/eval_jaxpr/convert_element_type | solution.py:129
  391.2 28.8 %dynamic_update_slice.42 = f32[2,512,12,64]{1,0,3,2:T(2,128)} dynamic-update-slice(f32[2,512,12,64]{1,0,3,2:T(2,128)} %get-tuple-element.677, f32[1,512,12,64]{1,0,3,2:T(1,128)S(1)} %copy.69, s32[]{:T(128)} %get-tuple-element.674, s32[]{:T(128)} %constant.82.clone.1..sunk, s32[]{:T(128)} %constant.82.clone.1..sunk, s32[]{:T(128)} %constant.82.clone.1..sunk) | dynamic-update-slice | bytes 3145732 | tf_op jit(solution)/shard_map/while/body/eval_jaxpr/while/body/jit(dynamic_update_index_in_dim)/dynamic_update_slice | solution.py:147
  427.1 11.4 %fusion.235 = f32[1024,64]{0,1:T(8,128)S(1)} fusion(f32[12,512]{1,0:T(8,128)S(1)} %copy-done.10, f32[512,12,1024]{2,0,1:T(8,128)} %fusion.230, pred[512,1024]{1,0:T(8,128)(4,1)S(1)} %copy-done.3, bf16[2,512,12,64]{1,3,2,0:T(8,128)(2,1)S(1)} %copy-done.13, s32[]{:T(128)} %get-tuple-element.674, f32[1024,64]{0,1:T(8,128)S(1)} %copy-done.18, ...), kind=kOutput, calls=%fused_computation.66.clone.1 | convolution fusion | flops 836894720 | bytes 27557892 | tf_op jit(solution)/shard_map/while/body/eval_jaxpr/while/body/eval_jaxpr/hqk,qhd->kd/dot_general | solution.py:122
  467.4 37.2 %fusion.75 = (bf16[1024,3072]{1,0:T(8,128)(2,1)}, f32[1024,3072]{1,0:T(8,128)}) fusion(f32[3072]{0:T(1024)S(1)} %convert_element_type.198, bf16[768,3072]{1,0:T(8,128)(2,1)} %all-gather.9.cloned.1.call-done, bf16[1,1024,768]{2,1,0:T(8,128)(2,1)S(1)} %copy-done.5, f32[768]{0:T(1024)S(1)} %convert_element_type.196, f32[768]{0:T(1024)S(1)} %convert_element_type.195, ...), kind=kOutput, calls=%fused_computation.94 | convolution fusion | flops 5044174848 | bytes 25192448 | tf_op jit(solution)/shard_map/dot_general | solution.py:266
  504.7 12.1 %convert_reduce_fusion = (f32[3072]{0:T(1024)}, bf16[1024,3072]{1,0:T(8,128)(2,1)S(1)}) fusion(f32[1024,3072]{1,0:T(8,128)} %get-tuple-element.431, f32[3072]{0:T(1024)S(1)} %convert_element_type.198, bf16[3072,768]{1,0:T(8,128)(2,1)} %all-gather.11.cloned.1.call-done, bf16[1,1024,768]{2,1,0:T(8,128)(2,1)} %param.25, f32[1024]{0:T(1024)S(1)} %copy-done.38), kind=kOutput, calls=%fused_computation.101 | convolution fusion | flops 4875088896 | bytes 25194496 | tf_op jit(solution)/shard_map/ne,fe->nf/dot_general | solution.py:350
  529.9 10.9 %fusion.158 = f32[3072,768]{1,0:T(8,128)} fusion(bf16[1024,3072]{1,0:T(8,128)(2,1)} %get-tuple-element.430, bf16[1,1024,768]{2,1,0:T(8,128)(2,1)S(1)} %copy-done.15, f32[1024]{0:T(1024)S(1)} %copy-done.38), kind=kOutput, calls=%fused_computation.221 | convolution fusion | flops 4834197504 | bytes 17305600 | tf_op jit(solution)/shard_map/nf,ne->fe/dot_general | solution.py:343
  542.2 114.6 %while.64 = (s32[]{:T(128)}, bf16[2,512,12,64]{1,3,2,0:T(8,128)(2,1)}, s32[2]{0:T(128)S(1)}, s32[]{:T(128)}, bf16[2,512,12,64]{1,3,2,0:T(8,128)(2,1)S(1)}, /*ind...) while((s32[]{:T(128)}, bf16[2,512,12,64]{1,3,2,0:T(8,128)(2,1)}, s32[2]{0:T(128)S(1)}, ...), condition=%wide.region_5.6_spmd, body=%wide.region_2.5_spmd.sunk | while | flops 1662388736 | bytes 103602792 | solution.py:105
  542.2 10.2 fusion.214
  554.7 33.5 %fusion.216 = (f32[12,512]{1,0:T(8,128)S(1)}, f32[12,512,1024]{2,1,0:T(8,128)}) fusion(f32[512,12,1024]{2,0,1:T(8,128)} %fusion.214, pred[512,1024]{1,0:T(8,128)(4,1)S(1)} %fusion.215), kind=kOutput, calls=%fused_computation.222.clone.1 | output fusion | flops 37749760 | bytes 50880512 | tf_op jit(solution)/shard_map/while/body/eval_jaxpr/while/body/eval_jaxpr/sub | solution.py:95
  588.2 11.2 %fusion.217 = bf16[2,512,12,64]{1,3,2,0:T(8,128)(2,1)} fusion(bf16[2,512,12,64]{1,3,2,0:T(8,128)(2,1)} %get-tuple-element.619, s32[]{:T(128)} %get-tuple-element.618, f32[12,512,1024]{2,1,0:T(8,128)} %get-tuple-element.585, f32[12,512]{1,0:T(8,128)S(1)} %get-tuple-element.586, bf16[1024,64]{0,1:T(8,128)(2,1)S(1)} %get-tuple-element.632), kind=kOutput, calls=%fused_computation.15.clone.1 | convolution fusion | flops 818282496 | bytes 26108416 | tf_op jit(solution)/shard_map/while/body/eval_jaxpr/while/body/eval_jaxpr/hqk,kd->qhd/dot_general | solution.py:98
  599.4 10.3 fusion.214
  612.0 33.4 %fusion.216 = (f32[12,512]{1,0:T(8,128)S(1)}, f32[12,512,1024]{2,1,0:T(8,128)}) fusion(f32[512,12,1024]{2,0,1:T(8,128)} %fusion.214, pred[512,1024]{1,0:T(8,128)(4,1)S(1)} %fusion.215), kind=kOutput, calls=%fused_computation.222.clone.1 | output fusion | flops 37749760 | bytes 50880512 | tf_op jit(solution)/shard_map/while/body/eval_jaxpr/while/body/eval_jaxpr/sub | solution.py:95
  645.4 11.2 %fusion.217 = bf16[2,512,12,64]{1,3,2,0:T(8,128)(2,1)} fusion(bf16[2,512,12,64]{1,3,2,0:T(8,128)(2,1)} %get-tuple-element.619, s32[]{:T(128)} %get-tuple-element.618, f32[12,512,1024]{2,1,0:T(8,128)} %get-tuple-element.585, f32[12,512]{1,0:T(8,128)S(1)} %get-tuple-element.586, bf16[1024,64]{0,1:T(8,128)(2,1)S(1)} %get-tuple-element.632), kind=kOutput, calls=%fused_computation.15.clone.1 | convolution fusion | flops 818282496 | bytes 26108416 | tf_op jit(solution)/shard_map/while/body/eval_jaxpr/while/body/eval_jaxpr/hqk,kd->qhd/dot_general | solution.py:98
  677.1 38.1 %all-reduce.18 = (f32[768]{0:T(1024)S(1)}, f32[128]{0:T(128)S(1)}, f32[768]{0:T(1024)S(1)}, f32[768]{0:T(1024)S(1)}, f32[768]{0:T(1024)S(1)}, /*index=5*/f32[768]{0:T(1024)S(1)}, f32[768]{0:T(1024)S(1)}, f32[3072]{0:T(1024)S(1)}) all-reduce(f32[768]{0:T(1024)S(1)} %reduce_sum.186, ...), channel_id=3, replica_groups=mesh['dp'=4,'fsdp'=8] {'dp','fsdp'}, use_global_device_ids=true, to_apply=%region_19.20.clone | all-reduce | flops 7808 | bytes 62464
  730.8 24.0 %reduce-scatter.10.cloned.1.call-done = f32[24,768]{1,0:T(8,128)} async-done(((f32[768,768]{1,0:T(8,128)}), f32[24,768]{1,0:T(8,128)}) %reduce-scatter.10.cloned.1.call-update) | async-done | bytes 73744 | tf_op jit(solution)/shard_map/reduce_scatter | solution.py:208
  754.8 142.1 %reduce-scatter.12.cloned.1.call-done = f32[24,3072]{1,0:T(8,128)} async-done(((f32[768,3072]{1,0:T(8,128)}), f32[24,3072]{1,0:T(8,128)}) %reduce-scatter.12.cloned.1.call-update) | async-done | bytes 294928 | tf_op jit(solution)/shard_map/reduce_scatter | solution.py:214
  896.9 141.2 %reduce-scatter.14.cloned.1.call-done = f32[96,768]{1,0:T(8,128)} async-done(((f32[3072,768]{1,0:T(8,128)}), f32[96,768]{1,0:T(8,128)}) %reduce-scatter.14.cloned.1.call-update) | async-done | bytes 294928 | tf_op jit(solution)/shard_map/reduce_scatter | solution.py:216
  (316 shorter events, 184.9 us)
Async XLA Ops:
  7.2 124.6 %copy-start.4 = (bf16[1,1024,768]{2,1,0:T(8,128)(2,1)S(1)}, bf16[1,1024,768]{2,1,0:T(8,128)(2,1)}, u32[]{:S(2)}) copy-start(bf16[1,1024,768]{2,1,0:T(8,128)(2,1)} %param.23) | copy-start | bytes 4718596
  7.2 57.0 %copy-start.49 = (bf16[24,128]{1,0:T(8,128)(2,1)S(1)}, bf16[24,128]{1,0:T(8,128)(2,1)}, u32[]{:S(2)}) copy-start(bf16[24,128]{1,0:T(8,128)(2,1)} %param.28) | copy-start | bytes 18436
  7.2 127.8 %all-gather.5.cloned.1.call-start = ((), (), s32[]{:S(2)}) async-start(), calls=%async_computation.5 | async-start | bytes 1216512 | tf_op jit(solution)/shard_map/all_gather | solution.py:170
  7.9 212.4 %all-gather.7.cloned.1.call-start = ((), (), s32[]{:S(2)}) async-start(), calls=%async_computation.6 | async-start | bytes 1216512 | tf_op jit(solution)/shard_map/all_gather | solution.py:174
  8.7 458.8 %all-gather.9.cloned.1.call-start = ((), (), s32[]{:S(2)}) async-start(), calls=%async_computation.7 | async-start | bytes 4866048 | tf_op jit(solution)/shard_map/all_gather | solution.py:180
  9.4 495.2 %all-gather.11.cloned.1.call-start = ((), (), s32[]{:S(2)}) async-start(), calls=%async_computation.8 | async-start | bytes 4866048 | tf_op jit(solution)/shard_map/all_gather | solution.py:182
  10.0 720.8 %reduce-scatter.16.cloned.1.call-start = ((), (), s32[]{:S(2)}) async-start(), calls=%async_computation.13 | async-start | bytes 405504
  10.1 122.8 %copy-start.51 = (f32[8]{0:T(128)}, f32[8]{0:T(128)S(1)}, u32[]{:S(2)}) copy-start(f32[8]{0:T(128)S(1)} %multiply_power_fusion) | copy-start | bytes 100
  60.2 74.8 %copy-start.40 = (f32[768]{0:T(1024)}, f32[768]{0:T(1024)S(1)}, u32[]{:S(2)}) copy-start(f32[768]{0:T(1024)S(1)} %convert_element_type.189) | copy-start | bytes 9220
  60.2 74.8 %copy-start.53 = (f32[768]{0:T(1024)}, f32[768]{0:T(1024)S(1)}, u32[]{:S(2)}) copy-start(f32[768]{0:T(1024)S(1)} %convert_element_type.190) | copy-start | bytes 9220
  61.9 73.1 %copy-start.33 = (f32[1024]{0:T(1024)}, f32[1024]{0:T(1024)S(1)}, u32[]{:S(2)}) copy-start(f32[1024]{0:T(1024)S(1)} %broadcast_multiply_fusion.4) | copy-start | bytes 12292
  63.9 74.2 %copy-start.43 = (f32[1024]{0:T(1024)}, f32[1024]{0:T(1024)S(1)}, u32[]{:S(2)}) copy-start(f32[1024]{0:T(1024)S(1)} %add_rsqrt_fusion) | copy-start | bytes 12292
  64.1 76.9 %copy-start.22 = (f32[1024,8]{0,1:T(8,128)}, f32[1024,8]{0,1:T(8,128)S(1)}, u32[]{:S(2)}) copy-start(f32[1024,8]{0,1:T(8,128)S(1)} %get-tuple-element.428) | copy-start | bytes 98308
  64.2 76.9 %copy-start.23 = (f32[1024,8]{0,1:T(8,128)}, f32[1024,8]{0,1:T(8,128)S(1)}, u32[]{:S(2)}) copy-start(f32[1024,8]{0,1:T(8,128)S(1)} %get-tuple-element.429) | copy-start | bytes 98308
  146.4 73.9 %copy-start.37 = (f32[1024]{0:T(1024)S(1)}, f32[1024]{0:T(1024)}, u32[]{:S(2)}) copy-start(f32[1024]{0:T(1024)} %fusion.146) | copy-start | bytes 12292
  159.2 16.1 %copy-start.1 = (f32[512,12,1024]{2,0,1:T(8,128)S(1)}, f32[512,12,1024]{2,0,1:T(8,128)}, u32[]{:S(2)}) copy-start(f32[512,12,1024]{2,0,1:T(8,128)} %get-tuple-element.595) | copy-start | bytes 75497472 | tf_op jit(solution)/shard_map/while/body/eval_jaxpr/while
  196.4 15.6 %copy-start.1 = (f32[512,12,1024]{2,0,1:T(8,128)S(1)}, f32[512,12,1024]{2,0,1:T(8,128)}, u32[]{:S(2)}) copy-start(f32[512,12,1024]{2,0,1:T(8,128)} %get-tuple-element.595) | copy-start | bytes 75497472 | tf_op jit(solution)/shard_map/while/body/eval_jaxpr/while
  245.0 19.5 %copy-start.2 = (pred[512,1024]{1,0:T(8,128)(4,1)}, pred[512,1024]{1,0:T(8,128)(4,1)S(1)}, u32[]{:S(2)}) copy-start(pred[512,1024]{1,0:T(8,128)(4,1)S(1)} %fusion.231) | copy-start | bytes 1572868 | tf_op jit(solution)/shard_map/while/body/eval_jaxpr/while
  245.8 18.7 %copy-start.9 = (f32[12,512]{1,0:T(8,128)}, f32[12,512]{1,0:T(8,128)S(1)}, u32[]{:S(2)}) copy-start(f32[12,512]{1,0:T(8,128)S(1)} %dynamic-slice_bitcast_fusion.2) | copy-start | bytes 73732 | tf_op jit(solution)/shard_map/while/body/eval_jaxpr/while
  348.4 19.4 %copy-start.2 = (pred[512,1024]{1,0:T(8,128)(4,1)}, pred[512,1024]{1,0:T(8,128)(4,1)S(1)}, u32[]{:S(2)}) copy-start(pred[512,1024]{1,0:T(8,128)(4,1)S(1)} %fusion.231) | copy-start | bytes 1572868 | tf_op jit(solution)/shard_map/while/body/eval_jaxpr/while
  349.2 18.6 %copy-start.9 = (f32[12,512]{1,0:T(8,128)}, f32[12,512]{1,0:T(8,128)S(1)}, u32[]{:S(2)}) copy-start(f32[12,512]{1,0:T(8,128)S(1)} %dynamic-slice_bitcast_fusion.2) | copy-start | bytes 73732 | tf_op jit(solution)/shard_map/while/body/eval_jaxpr/while
  439.4 10.6 %copy-start.8 = (f32[1024,64]{0,1:T(8,128)}, f32[1024,64]{0,1:T(8,128)S(1)}, u32[]{:S(2)}) copy-start(f32[1024,64]{0,1:T(8,128)S(1)} %get-tuple-element.227) | copy-start | bytes 786436
  441.1 8.7 copy-start.52
  453.9 277.0 %reduce-scatter.8.cloned.1.call-start = ((), (), s32[]{:S(2)}) async-start(), calls=%async_computation.9 | async-start | bytes 2433024 | tf_op jit(solution)/shard_map/reduce_scatter | solution.py:204
  460.6 294.2 %reduce-scatter.10.cloned.1.call-start = ((), (), s32[]{:S(2)}) async-start(), calls=%async_computation.10 | async-start | bytes 2433024 | tf_op jit(solution)/shard_map/reduce_scatter | solution.py:208
  460.7 56.1 %copy-start.46 = (f32[768]{0:T(1024)}, f32[768]{0:T(1024)S(1)}, u32[]{:S(2)}) copy-start(f32[768]{0:T(1024)S(1)} %convert_element_type.195) | copy-start | bytes 9220
  467.4 429.5 %reduce-scatter.12.cloned.1.call-start = ((), (), s32[]{:S(2)}) async-start(), calls=%async_computation.11 | async-start | bytes 9732096 | tf_op jit(solution)/shard_map/reduce_scatter | solution.py:214
  528.1 509.9 %reduce-scatter.14.cloned.1.call-start = ((), (), s32[]{:S(2)}) async-start(), calls=%async_computation.12 | async-start | bytes 9732096 | tf_op jit(solution)/shard_map/reduce_scatter | solution.py:216
  542.2 115.5 %copy-start.36 = (f32[12,64]{1,0:T(8,128)S(1)}, f32[12,64]{1,0:T(8,128)}, u32[]{:S(2)}) copy-start(f32[12,64]{1,0:T(8,128)} %get-tuple-element.410) | copy-start | bytes 9220
  715.2 322.8 %copy-start.66 = (f32[24]{0:T(128)}, f32[24]{0:T(128)S(1)}, u32[]{:S(2)}) copy-start(f32[24]{0:T(128)S(1)} %dynamic-slice.4) | copy-start | bytes 292
  719.3 8.6 copy-start.57
  719.3 8.6 copy-start.62
  (57 other events, 232.6 us)
Sparse Core Ops, SparseCore 0:
  11.0 57.1 all-gather.4
  71.2 53.0 all-gather.6
  127.3 62.6 all-gather.8
  192.8 62.5 all-gather.10
  454.0 92.1 reduce-scatter.15
  552.7 98.0 reduce-scatter.7
  656.7 98.0 reduce-scatter.9
  762.3 134.5 reduce-scatter.11
  903.4 134.6 reduce-scatter.13
where the time goes:
time: 1060 us; the launch traced here: 1050 us
  waiting for transfers between devices  310 us (29%)
  matrix products  290 us (27%)
  other arithmetic  155 us (15%)
  blocking collectives  148 us (14%)
  local copies, waits for them, and re-layouts  125 us (12%)
  between operations  15.6 us (1%)
    reduce_scatter x1, waiting for transfers between devices, spread(): lax.psum_scatter(up_weight, ('dp', 'fsdp'), scatter_dimension=0, tiled=True)  142 us
    reduce_scatter x1, waiting for transfers between devices, spread(): lax.psum_scatter(down_weight, ('dp', 'fsdp'), scatter_dimension=0, tiled=...  141 us
    unnamed x2, blocking collectives  80.6 us
    all_gather x1, blocking collectives, collect(): lax.all_gather(keyval_weight, ('dp', 'fsdp'), axis=0, tiled=True)  67.6 us
    sub x2, other arithmetic, one_block(): exponent = jnp.exp(scores - row_max)  66.9 us
    dot_general x6, matrix products, block_scores(): jnp.einsum('qhd,kd->hqk', query_block, key_rot, preferred_element_type=jn...  62 us
    dynamic_update_slice x4, local copies, waits for them, and re-layouts, attend_backward(): lax.scan(one_block, (zero_rows, zero_rows), (query_blocks, grad_blocks, l...  60.9 us
    dot_general x4, matrix products, one_block(): jnp.einsum('hqk,kd->qhd', softmax_low, values, preferred_element_type=jnp...  39.2 us
  transfers between devices with their start and end apart: 9, of which 3 were waited for; matrix products, arithmetic and copies ran while one was open for 53% of the time, Pallas kernels for 0%

commit v1 on v0

v1 whole, which is shorter than its diff:
```python
import functools

import jax
import jax.numpy as jnp
from jax import lax
from jax.experimental import pallas as pl
from jax.experimental.pallas import tpu as pltpu
from jax.sharding import PartitionSpec as P

f32 = jnp.float32
bf16 = jnp.bfloat16

ROT = 16
EPS = 1e-05
NEG = -1e30
ROOT_HALF = 0.7071067811865476
INV_ROOT_TAU = 0.3989422804014327
LANES = 128
BOTH = ("dp", "fsdp")
VMEM = 60 * 1024 * 1024

QB, OB, GA, BA, GM, BM, DB, UB, KB = 0, 1, 2, 3, 4, 5, 6, 7, 11


def dot(a, b, ca, cb):
    return lax.dot_general(a, b, (((ca,), (cb,)), ((), ())), preferred_element_type=f32)


def params(**kw):
    return pltpu.CompilerParams(vmem_limit_bytes=VMEM, **kw)


def whole(shape):
    return pl.BlockSpec(shape, lambda *_: (0,) * len(shape))


def rotary_tables(seq_len, head_dim):
    half = ROT // 2
    inverse_freq = 10000.0 ** (-(2.0 * jnp.arange(half, dtype=f32)) / ROT)
    angles = jnp.arange(seq_len, dtype=f32)[:, None] * inverse_freq[None, :]
    cos, sin = jnp.cos(angles), jnp.sin(angles)
    one = jnp.ones((seq_len, head_dim - ROT), f32)
    zero = jnp.zeros((seq_len, half), f32)
    none = jnp.zeros((seq_len, head_dim - ROT), f32)
    own = jnp.concatenate([cos, cos, one], 1)
    up = jnp.concatenate([sin, zero, none], 1)
    down = jnp.concatenate([zero, sin, none], 1)
    two = lambda t: jnp.concatenate([t, t], 1)
    return jnp.stack([two(own), two(up), two(down)])


def partners(v):
    half = ROT // 2
    return pltpu.roll(v, LANES - half, 1), pltpu.roll(v, half, 1)


def rotate(v, own, up, down):
    ahead, behind = partners(v)
    return v * own - ahead * up + behind * down


def rotate_back(v, own, up, down):
    ahead, behind = partners(v)
    return v * own + ahead * up - behind * down


def standardise(rows):
    average = jnp.mean(rows, axis=-1, keepdims=True)
    centred = rows - average
    scaled = lax.rsqrt(jnp.mean(centred * centred, axis=-1, keepdims=True) + EPS)
    return centred * scaled, scaled


def norm_back(grad, normed, scaled, gain):
    e = grad * gain
    return scaled * (
        e - jnp.mean(e, axis=-1, keepdims=True) - normed * jnp.mean(e * normed, axis=-1, keepdims=True)
    )


def col_sum(v):
    return jnp.sum(v, axis=0, keepdims=True)


def kept_rows(block, rows, length):
    pos = lax.broadcasted_iota(jnp.int32, (rows, 1), 0) + block * rows
    return (pos < length).astype(f32)


def spread_key_bias(width, kv_width, per_row, per_kv):
    row = lax.broadcasted_iota(jnp.int32, (width, kv_width), 0)
    col = lax.broadcasted_iota(jnp.int32, (width, kv_width), 1)
    owner = col // per_kv
    return (row == owner * per_row + (col - owner * per_kv)).astype(bf16)


def pre_kernel(len_ref, x_ref, cot_ref, w_ref, tab_ref, q_ref, kv_ref, ha_ref, hm_ref, gy_ref, gm_ref, vec_ref, vec_s, *, dims):
    width, kv_width, rows, per_row, per_kv = dims
    i = pl.program_id(0)
    c_out = width + kv_width
    c_vec = c_out + width

    @pl.when(i == 0)
    def _():
        low = w_ref[:, c_vec : c_vec + LANES]
        lines = low.astype(f32).T[:16]
        vec_s[:16, :] = lines
        spread = spread_key_bias(width, kv_width, per_row, per_kv)
        vec_s[16:32, :kv_width] = dot(lines.astype(bf16), spread, 1, 0)
        vec_ref[...] = vec_s[...]

    normed, _ = standardise(x_ref[...].astype(f32))
    vec = vec_s[...]
    ha = (normed * vec[GA : GA + 1] + vec[BA : BA + 1]).astype(bf16)
    hm = (normed * vec[GM : GM + 1] + vec[BM : BM + 1]).astype(bf16)
    ha_ref[...] = ha
    hm_ref[...] = hm
    own, up, down = tab_ref[0], tab_ref[1], tab_ref[2]
    scale = (kv_width // 2) ** -0.5
    for p in range(width // LANES):
        cols = slice(p * LANES, (p + 1) * LANES)
        lin = dot(ha, w_ref[:, cols], 1, 0) + vec[QB : QB + 1, cols]
        rot = rotate(lin, own, up, down).astype(bf16)
        q_ref[:, cols] = (rot.astype(f32) * scale).astype(bf16)
    lin = dot(ha, w_ref[:, width:c_out], 1, 0) + vec[16 + KB : 17 + KB, :kv_width]
    lane = lax.broadcasted_iota(jnp.int32, (rows, kv_width), 1)
    kv_ref[...] = jnp.where(lane < kv_width // 2, rotate(lin, own, up, down), lin).astype(bf16)
    keep = kept_rows(i, rows, len_ref[0])
    gy = (cot_ref[...].astype(f32) * keep).astype(bf16)
    gy_ref[...] = gy
    gm_ref[...] = dot(gy, w_ref[:, c_out:c_vec], 1, 1).astype(bf16)


def pre(length, x, cot, w1, tables, kv_width, shards):
    tokens, width = x.shape
    rows = 256
    blk = pl.BlockSpec((rows, width), lambda i, *_: (i, 0))
    kvb = pl.BlockSpec((rows, kv_width), lambda i, *_: (i, 0))
    dims = (width, kv_width, rows, width // shards, kv_width // shards)
    wide = jax.ShapeDtypeStruct((tokens, width), bf16)
    return pl.pallas_call(
        functools.partial(pre_kernel, dims=dims),
        grid_spec=pltpu.PrefetchScalarGridSpec(
            num_scalar_prefetch=1,
            grid=(tokens // rows,),
            in_specs=[blk, blk, whole(w1.shape), pl.BlockSpec((3, rows, LANES), lambda i, *_: (0, i, 0))],
            out_specs=[blk, kvb, blk, blk, blk, blk, whole((32, width))],
            scratch_shapes=[pltpu.VMEM((32, width), f32)],
        ),
        out_shape=[
            wide,
            jax.ShapeDtypeStruct((tokens, kv_width), bf16),
            wide,
            wide,
            wide,
            wide,
            jax.ShapeDtypeStruct((32, width), f32),
        ],
        compiler_params=params(),
        name="pre",
    )(length, x, cot, w1, tables)


def attn_kernel(len_ref, q_ref, gm_ref, kv_ref, tab_ref, mix_ref, dq_ref, dkv_ref, k0, k1, v0, v1, acc, *, qb):
    p = pl.program_id(0)
    tokens, kv_width = kv_ref.shape
    head = kv_width // 2

    @pl.when(p == 0)
    def _():
        kv = kv_ref[...]
        zero = jnp.zeros((tokens, head), bf16)
        k, v = kv[:, :head], kv[:, head:]
        k0[...] = jnp.concatenate([k, zero], 1)
        k1[...] = jnp.concatenate([zero, k], 1)
        v0[...] = jnp.concatenate([v, zero], 1)
        v1[...] = jnp.concatenate([zero, v], 1)
        acc[...] = jnp.zeros_like(acc)

    last = len_ref[0] - 1
    lane = lax.broadcasted_iota(jnp.int32, (qb, LANES), 1)
    scale = head**-0.5
    for i in range(tokens // qb):
        r = pl.ds(i * qb, qb)
        kn = (i + 1) * qb
        q, gm = q_ref[r, :], gm_ref[r, :]
        q_t, gm_t = q.T, gm.T
        col = lax.broadcasted_iota(jnp.int32, (qb, kn), 1)
        limit = jnp.minimum(lax.broadcasted_iota(jnp.int32, (qb, 1), 0) + i * qb, last)
        allowed = col <= limit
        mixed = jnp.zeros((qb, LANES), f32)
        probs = []
        for h, (k, v) in enumerate(((k0, v0), (k1, v1))):
            s = jnp.where(allowed, dot(q, k[:kn, :], 1, 1), NEG)
            e = jnp.exp(s - jnp.max(s, axis=1, keepdims=True))
            pr = e * (1.0 / jnp.sum(e, axis=1, keepdims=True))
            low = pr.astype(bf16)
            mixed = mixed + dot(low, v[:kn, :], 1, 0)
            acc[head:, :kn] += dot(gm_t[head * h : head * (h + 1), :], low, 1, 0)
            probs.append(pr)
        mix_ref[r, :] = mixed.astype(bf16)
        inner = gm.astype(f32) * mixed
        first = jnp.sum(jnp.where(lane < head, inner, 0.0), axis=1, keepdims=True)
        second = jnp.sum(jnp.where(lane < head, 0.0, inner), axis=1, keepdims=True)
        dq = jnp.zeros((qb, LANES), f32)
        for h, (k, v, row) in enumerate(((k0, v0, first), (k1, v1, second))):
            ds = (probs[h] * (dot(gm, v[:kn, :], 1, 1) - row)).astype(bf16)
            dq = dq + dot(ds, k[:kn, :], 1, 0)
            acc[:head, :kn] += dot(q_t[head * h : head * (h + 1), :], ds, 1, 0)
        dq_ref[r, :] = rotate_back(dq * scale, tab_ref[0, r, :], tab_ref[1, r, :], tab_ref[2, r, :]).astype(bf16)

    @pl.when(p == pl.num_programs(0) - 1)
    def _():
        dkv = acc[...].T
        lanes = lax.broadcasted_iota(jnp.int32, (tokens, kv_width), 1)
        back = rotate_back(dkv, tab_ref[0], tab_ref[1], tab_ref[2])
        dkv_ref[...] = jnp.where(lanes < head, back, dkv).astype(bf16)


def attention(length, q, gm, kv, tables):
    tokens, width = q.shape
    kv_width = kv.shape[1]
    blk = pl.BlockSpec((tokens, LANES), lambda p, *_: (0, p))
    wide = jax.ShapeDtypeStruct((tokens, width), bf16)
    return pl.pallas_call(
        functools.partial(attn_kernel, qb=256),
        grid_spec=pltpu.PrefetchScalarGridSpec(
            num_scalar_prefetch=1,
            grid=(width // LANES,),
            in_specs=[blk, blk, whole((tokens, kv_width)), whole((3, tokens, LANES))],
            out_specs=[blk, blk, whole((tokens, kv_width))],
            scratch_shapes=[pltpu.VMEM((tokens, LANES), bf16)] * 4 + [pltpu.VMEM((kv_width, tokens), f32)],
        ),
        out_shape=[wide, wide, jax.ShapeDtypeStruct((tokens, kv_width), bf16)],
        compiler_params=params(),
        name="attention",
    )(length, q, gm, kv, tables)


def post_kernel(len_ref, x_ref, cot_ref, ha_ref, gy_ref, mix_ref, dq_ref, dkv_ref, w_ref, vec_ref, out_ref, gt_ref, dw_ref, acc, sums, *, dims):
    width, kv_width, rows, per_row, per_kv = dims
    i = pl.program_id(0)
    c_out = width + kv_width
    c_vec = c_out + width

    @pl.when(i == 0)
    def _():
        acc[...] = jnp.zeros_like(acc)
        sums[...] = jnp.zeros_like(sums)

    keep = kept_rows(i, rows, len_ref[0])
    vec = vec_ref[...]
    x = x_ref[...].astype(f32)
    mixed, gy, ha, dq, dkv = mix_ref[...], gy_ref[...], ha_ref[...], dq_ref[...], dkv_ref[...]
    attn_out = dot(mixed, w_ref[:, c_out:c_vec], 1, 0) + vec[OB : OB + 1]
    out_ref[...] = x + keep * attn_out
    acc[:, :width] += dot(ha, dq, 0, 0)
    acc[:, width:c_out] += dot(ha, dkv, 0, 0)
    acc[:, c_out:c_vec] += dot(mixed, gy, 0, 0)
    grad = dot(dq, w_ref[:, :width], 1, 1) + dot(dkv, w_ref[:, width:c_out], 1, 1)
    normed, scaled = standardise(x)
    gt_ref[...] = cot_ref[...].astype(f32) + norm_back(grad, normed, scaled, vec[GA : GA + 1])
    sums[QB : QB + 1] += col_sum(dq.astype(f32))
    sums[OB : OB + 1] += col_sum(gy.astype(f32))
    sums[GA : GA + 1] += col_sum(grad * normed)
    sums[BA : BA + 1] += col_sum(grad)
    sums[8:9, :kv_width] += col_sum(dkv.astype(f32))

    @pl.when(i == pl.num_programs(0) - 1)
    def _():
        dw_ref[:, :c_vec] = acc[...].astype(bf16)
        spread = spread_key_bias(width, kv_width, per_row, per_kv)
        low = sums[...].astype(bf16)
        key = dot(low[8:16, :kv_width], spread, 1, 1)
        row = lax.broadcasted_iota(jnp.int32, (16, width), 0)
        both = jnp.where(row == 8, jnp.concatenate([key, key], 0), low.astype(f32))
        both = jnp.concatenate([both, jnp.zeros((LANES - 16, width), f32)], 0)
        dw_ref[:, c_vec:] = both.T.astype(bf16)


def post(length, x, cot, ha, gy, mixed, dq, dkv, w1, vec, shards):
    tokens, width = x.shape
    kv_width = dkv.shape[1]
    rows = 256
    blk = pl.BlockSpec((rows, width), lambda i, *_: (i, 0))
    kvb = pl.BlockSpec((rows, kv_width), lambda i, *_: (i, 0))
    dims = (width, kv_width, rows, width // shards, kv_width // shards)
    full = jax.ShapeDtypeStruct((tokens, width), f32)
    return pl.pallas_call(
        functools.partial(post_kernel, dims=dims),
        grid_spec=pltpu.PrefetchScalarGridSpec(
            num_scalar_prefetch=1,
            grid=(tokens // rows,),
            in_specs=[blk, blk, blk, blk, blk, blk, kvb, whole(w1.shape), whole(vec.shape)],
            out_specs=[blk, blk, whole(w1.shape)],
            scratch_shapes=[pltpu.VMEM((width, w1.shape[1] - LANES), f32), pltpu.VMEM((16, width), f32)],
        ),
        out_shape=[full, full, jax.ShapeDtypeStruct(w1.shape, bf16)],
        compiler_params=params(),
        name="post",
    )(length, x, cot, ha, gy, mixed, dq, dkv, w1, vec)


def ff_kernel(len_ref, hm_ref, gy_ref, wu_ref, wd_ref, vec_ref, x_ref, base_ref, gt_ref, out_ref, gtok_ref, dwu_ref, dwd_ref, dv_ref, act_s, gup_s, mlp, gh, sums, *, rows):
    j = pl.program_id(0)
    tokens, width = hm_ref.shape
    blocks = tokens // rows

    @pl.when(j == 0)
    def _():
        mlp[...] = jnp.zeros_like(mlp)
        gh[...] = jnp.zeros_like(gh)
        sums[...] = jnp.zeros_like(sums)

    bias = vec_ref[pl.ds(UB + j, 1), :]
    total = jnp.zeros((1, wu_ref.shape[1]), f32)
    for i in range(blocks):
        r = pl.ds(i * rows, rows)
        u = dot(hm_ref[r, :], wu_ref[...], 1, 0) + bias
        cdf = 0.5 * (1.0 + lax.erf(u * ROOT_HALF))
        pdf = jnp.exp(-0.5 * u * u) * INV_ROOT_TAU
        act = (u * cdf).astype(bf16)
        act_s[r, :] = act
        grad = (dot(gy_ref[r, :], wd_ref[...], 1, 1) * (cdf + u * pdf)).astype(bf16)
        gup_s[r, :] = grad
        total = total + col_sum(grad.astype(f32))
        mlp[r, :] += dot(act, wd_ref[...], 1, 0)
        gh[r, :] += dot(grad, wu_ref[...], 1, 1)
    sums[pl.ds(j, 1), :] = total
    dwd_ref[...] = dot(act_s[...], gy_ref[...], 0, 0).astype(bf16)
    dwu_ref[...] = dot(hm_ref[...], gup_s[...], 0, 0).astype(bf16)

    @pl.when(j == pl.num_programs(0) - 1)
    def _():
        gain = vec_ref[GM : GM + 1]
        down_bias = vec_ref[DB : DB + 1]
        d_gain = jnp.zeros((1, width), f32)
        d_shift = jnp.zeros((1, width), f32)
        for i in range(blocks):
            r = pl.ds(i * rows, rows)
            keep = kept_rows(i, rows, len_ref[0])
            out_ref[r, :] = (base_ref[r, :] + keep * (mlp[r, :] + down_bias)).astype(bf16)
            normed, scaled = standardise(x_ref[r, :].astype(f32))
            grad = gh[r, :]
            gtok_ref[r, :] = gt_ref[r, :] + norm_back(grad, normed, scaled, gain)
            d_gain = d_gain + col_sum(grad * normed)
            d_shift = d_shift + col_sum(grad)
        blocks_up = pl.num_programs(0)
        sums[4:5, :] = d_gain
        sums[5:6, :] = d_shift
        both = jnp.concatenate([sums[...], jnp.zeros((LANES - 8, width), f32)], 0)
        dv_ref[...] = both.T.astype(bf16)


def feed_forward(length, hm, gy, w2, vec, x, base, gt):
    tokens, width = x.shape
    blocks = w2.shape[1] // (2 * width)
    one = lambda s: pl.BlockSpec(s, lambda *_: (0, 0), pipeline_mode=pl.Buffered(1))
    up = pl.BlockSpec((width, width), lambda j, *_: (0, j))
    dn = pl.BlockSpec((width, width), lambda j, *_: (0, j + blocks))
    tok = (tokens, width)
    half = jax.ShapeDtypeStruct((width, blocks * width), bf16)
    return pl.pallas_call(
        functools.partial(ff_kernel, rows=256),
        grid_spec=pltpu.PrefetchScalarGridSpec(
            num_scalar_prefetch=1,
            grid=(blocks,),
            in_specs=[one(tok), one(tok), up, dn, one(vec.shape), one(tok), one(tok), one(tok)],
            out_specs=[whole(tok), whole(tok), up, up, whole((width, LANES))],
            scratch_shapes=[
                pltpu.VMEM((tokens, width), bf16),
                pltpu.VMEM((tokens, width), bf16),
                pltpu.VMEM(tok, f32),
                pltpu.VMEM(tok, f32),
                pltpu.VMEM((8, width), f32),
            ],
        ),
        out_shape=[
            jax.ShapeDtypeStruct(tok, bf16),
            jax.ShapeDtypeStruct(tok, f32),
            half,
            half,
            jax.ShapeDtypeStruct((width, LANES), bf16),
        ],
        compiler_params=params(),
        name="feed_forward",
    )(length, hm, gy, w2, w2, vec, x, base, gt)


def bits_of(axis, size):
    return [(axis, b) for b in range(size.bit_length() - 1)]


def swap(v, axis, bit):
    size = lax.axis_size(axis)
    return lax.ppermute(v, axis, [(i, i ^ (1 << bit)) for i in range(size)])


def gather_rows(v, order, index_order):
    rows, cols = v.shape
    cur = v.reshape((1,) * len(index_order) + v.shape)
    for axis, bit in order:
        got = swap(cur.reshape(-1, cols), axis, bit).reshape(cur.shape)
        here = (lax.axis_index(axis) >> bit) & 1
        where = index_order.index((axis, bit))
        low = jnp.where(here == 0, cur, got)
        high = jnp.where(here == 0, got, cur)
        cur = jnp.concatenate([low, high], where)
    return cur.reshape(-1, cols)


def body(
    tokens,
    lengths,
    cotangent,
    query_weight,
    query_bias,
    keyval_weight,
    keyval_bias,
    out_weight,
    out_bias,
    norm_attn_gain,
    norm_attn_bias,
    norm_mlp_gain,
    norm_mlp_bias,
    up_weight,
    up_bias,
    down_weight,
    down_bias,
):
    n_dp, n_fsdp = lax.axis_size("dp"), lax.axis_size("fsdp")
    shards = n_dp * n_fsdp
    rows, width = query_weight.shape
    kv_width = keyval_weight.shape[1]
    ff = up_weight.shape[1]
    blocks = ff // width
    seq_len = tokens.shape[1]
    x = tokens.reshape(seq_len, width)
    cot = cotangent.reshape(seq_len, width)

    up_local = up_weight.reshape(rows, shards, blocks, rows).transpose(0, 2, 1, 3).reshape(rows, ff)
    dn_local = down_weight.reshape(blocks, rows, width).transpose(1, 0, 2).reshape(rows, ff)
    w2 = lax.all_gather(jnp.concatenate([up_local, dn_local], 1), BOTH, axis=0, tiled=True)

    up_bias_cols = up_bias.reshape(blocks, rows)
    key_bias_col = jnp.pad(keyval_bias, (0, rows - keyval_bias.shape[0]))
    vecs = [query_bias, out_bias, norm_attn_gain, norm_attn_bias, norm_mlp_gain, norm_mlp_bias, down_bias]
    vecs = jnp.concatenate([jnp.stack(vecs), up_bias_cols, key_bias_col[None]], 0)
    vecs = jnp.pad(vecs, ((0, LANES - vecs.shape[0]), (0, 0))).T
    local = jnp.concatenate([query_weight, keyval_weight, out_weight, vecs], 1)
    dp_bits, fs_bits = bits_of("dp", n_dp), bits_of("fsdp", n_fsdp)
    index_order = dp_bits[::-1] + fs_bits[::-1]
    order = fs_bits[:0:-1] + dp_bits[:0:-1] + fs_bits[:1] + dp_bits[:1]
    w1 = gather_rows(local, order, index_order)

    tables = rotary_tables(seq_len, kv_width // 2)
    q, kv, ha, hm, gy, gm, vec = pre(lengths, x, cot, w1, tables, kv_width, shards)
    mixed, dq, dkv = attention(lengths, q, gm, kv, tables)
    base, gt, dw1 = post(lengths, x, cot, ha, gy, mixed, dq, dkv, w1, vec, shards)
    own1 = lax.psum_scatter(dw1, BOTH, scatter_dimension=0, tiled=True)
    layer_out, gtok, dwu, dwd, dv = feed_forward(lengths, hm, gy, w2, vec, x, base, gt)
    own2 = lax.psum_scatter(jnp.concatenate([dwu, dwd, dv], 1), BOTH, scatter_dimension=0, tiled=True)

    own1, own2 = own1.astype(f32), own2.astype(f32)
    c_out = width + kv_width
    c_vec = c_out + width
    v1 = own1[:, c_vec:].T
    v2 = own2[:, 2 * ff :].T
    g_up = own2[:, :ff].reshape(rows, blocks, shards, rows).transpose(0, 2, 1, 3).reshape(rows, ff)
    g_dn = own2[:, ff : 2 * ff].reshape(rows, blocks, width).transpose(1, 0, 2).reshape(blocks * rows, width)
    return (
        layer_out.reshape(tokens.shape),
        gtok.reshape(tokens.shape),
        own1[:, :width],
        v1[QB],
        own1[:, width:c_out],
        v1[8, : kv_width // shards],
        own1[:, c_out:c_vec],
        v1[OB],
        v1[GA],
        v1[BA],
        v2[4],
        v2[5],
        g_up,
        v2[:4].reshape(-1),
        g_dn,
        v1[OB],
    )


def solution(mesh):
    mat, vec, seq = P(BOTH, None), P(BOTH), P(BOTH, None, None)
    return jax.shard_map(
        body,
        mesh=mesh,
        in_specs=(seq, vec, seq, mat, vec, mat, vec, mat, vec, vec, vec, vec, vec, mat, vec, mat, vec),
        out_specs=(seq, seq, mat, vec, mat, vec, mat, vec, vec, vec, vec, vec, mat, vec, mat, vec),
        check_vma=False,
    )
```

time: 1060 us -> 409 us (0.39); the launches traced: 1050 us -> 408 us
  matrix products: 290 us -> 0 us
  blocking collectives: 148 us -> 0 us
  other arithmetic: 155 us -> 17.9 us
  Pallas kernels: 0 us -> 114 us
  local copies, waits for them, and re-layouts: 125 us -> 26.2 us
  waiting for transfers between devices: 310 us -> 226 us
    dot_general x33 -> x0, matrix products: 290 us -> none  [the longest x6 62 us: block_scores(): jnp.einsum('qhd,kd->hqk', query_block, key_rot, preferred_element_type=jn...]
    reduce_scatter x4 -> x1, waiting for transfers between devices: 307 us -> 53.5 us  [body(): own1 = lax.psum_scatter(dw1, BOTH, scatter_dimension=0, tiled=True)]
    unnamed x10 -> x4, waiting for transfers between devices: 2.66 us -> 136 us
    pallas_call x0 -> x4, Pallas kernels: none -> 114 us  [the longest x1 47.4 us: attention(): pl.pallas_call(functools.partial(attn_kernel, qb=256), grid_spec=pltpu.Pr...]
    unnamed x2 -> x0, blocking collectives: 80.6 us -> none
    all_gather x1 -> x0, blocking collectives: 67.6 us -> none  [collect(): lax.all_gather(keyval_weight, ('dp', 'fsdp'), axis=0, tiled=True)]
    sub x2 -> x0, other arithmetic: 66.9 us -> none  [one_block(): exponent = jnp.exp(scores - row_max)]
    dynamic_update_slice x4 -> x0, local copies, waits for them, and re-layouts: 60.9 us -> none  [attend_backward(): lax.scan(one_block, (zero_rows, zero_rows), (query_blocks, grad_blocks, l...]
  transfers between devices with their start and end apart: 9 -> 8, of which waited for: 3 -> 6; matrix products, arithmetic and copies ran while one was open for 53% -> 7% of each run, Pallas kernels for 0% -> 28%
where the time goes in v1:
time: 409 us; the launch traced here: 408 us
  waiting for transfers between devices  226 us (55%)
  Pallas kernels  114 us (28%)
  local copies, waits for them, and re-layouts  26.2 us (6%)
  other arithmetic  17.9 us (4%)
  between operations  14.8 us (4%)
  starting transfers between devices  9.13 us (2%)
    unnamed x4, waiting for transfers between devices  136 us
    reduce_scatter x1, waiting for transfers between devices, body(): own1 = lax.psum_scatter(dw1, BOTH, scatter_dimension=0, tiled=True)  53.5 us
    pallas_call x1, Pallas kernels, attention(): pl.pallas_call(functools.partial(attn_kernel, qb=256), grid_spec=pltpu.Pr...  47.4 us
    pallas_call x1, Pallas kernels, feed_forward(): pl.pallas_call(functools.partial(ff_kernel, rows=256), grid_spec=pltpu.Pr...  42.6 us
    ppermute x5, waiting for transfers between devices, swap(): return lax.ppermute(v, axis, [(i, i ^ 1 << bit) for i in range(size)])  36.4 us
    pallas_call x1, Pallas kernels, post(): pl.pallas_call(functools.partial(post_kernel, dims=dims), grid_spec=pltpu...  13.8 us
    pallas_call x1, Pallas kernels, pre(): pl.pallas_call(functools.partial(pre_kernel, dims=dims), grid_spec=pltpu....  10.1 us
    concatenate x1, other arithmetic, body(): jnp.concatenate([dwu, dwd, dv], 1)  9.32 us
  transfers between devices with their start and end apart: 8, of which 6 were waited for; matrix products, arithmetic and copies ran while one was open for 7% of the time, Pallas kernels for 28%

profile of v1, /device:TPU:0, one launch (start us, length us, event | category | flops | bytes accessed | tf_op | source)
XLA Modules:
  0.0 408.1 jit_solution(13428160758470929153)
XLA Ops:
  7.2 1.0 copy.82
  8.2 2.1 reshape.1049
  10.7 1.3 reshape.1050
  13.2 4.1 %collective-permute-start = (bf16[24,1792]{1,0:T(8,128)(2,1)S(1)}, bf16[24,1792]{1,0:T(8,128)(2,1)S(1)}, u32[]{:S(2)}, u32[]{:S(2)}) collective-permute-start(bf16[24,1792]{1,0:T(8,128)(2,1)S(1)} %pad_maximum_fusion.14), channel_id=1, source_target_pairs={{0,4},{1,5},{2,6},{3,7},{4,0},{5,1},{6,2},{7,3},{8,12},{9,13},{10,... | collective-permute-start | bytes 258056 | tf_op jit(solution)/shard_map/ppermute | solution.py:396
  17.3 4.4 %collective-permute-done = bf16[24,1792]{1,0:T(8,128)(2,1)S(1)} collective-permute-done((bf16[24,1792]{1,0:T(8,128)(2,1)S(1)}, bf16[24,1792]{1,0:T(8,128)(2,1)S(1)}, u32[]{:S(2)}, u32[]{:S(2)}) %collective-permute-start) | collective-permute-done | bytes 86048 | tf_op jit(solution)/shard_map/ppermute | solution.py:396
  22.5 5.9 %collective-permute-done.1 = bf16[48,1792]{1,0:T(8,128)(2,1)S(1)} collective-permute-done((bf16[48,1792]{1,0:T(8,128)(2,1)S(1)}, bf16[48,1792]{1,0:T(8,128)(2,1)S(1)}, u32[]{:S(2)}, u32[]{:S(2)}) %collective-permute-start.1) | collective-permute-done | bytes 172064 | tf_op jit(solution)/shard_map/ppermute | solution.py:396
  28.5 2.4 collective-permute-start.2
  31.0 5.4 %collective-permute-done.2 = bf16[96,1792]{1,0:T(8,128)(2,1)S(1)} collective-permute-done((bf16[96,1792]{1,0:T(8,128)(2,1)S(1)}, bf16[96,1792]{1,0:T(8,128)(2,1)S(1)}, u32[]{:S(2)}, u32[]{:S(2)}) %collective-permute-start.2) | collective-permute-done | bytes 344096 | tf_op jit(solution)/shard_map/ppermute | solution.py:396
  36.6 1.7 collective-permute-start.3
  38.4 20.7 %collective-permute-done.3 = bf16[192,1792]{1,0:T(8,128)(2,1)S(1)} collective-permute-done((bf16[192,1792]{1,0:T(8,128)(2,1)S(1)}, bf16[192,1792]{1,0:T(8,128)(2,1)S(1)}, u32[]{:S(2)}, u32[]{:S(2)}) %collective-permute-start.3) | collective-permute-done | bytes 688160 | tf_op jit(solution)/shard_map/ppermute | solution.py:396
  59.3 1.2 copy.77
  60.5 1.9 fusion.3
  62.5 1.7 concatenate.307
  64.3 1.7 concatenate.306
  66.7 1.7 concatenate.305
  68.5 2.3 pad_maximum_fusion.2.tab_ref
  71.0 1.6 broadcast_select_fusion.1
  72.8 1.8 copy.80
  74.6 10.1 %pre.1 = (bf16[1024,768]{1,0:T(8,128)(2,1)}, bf16[1024,128]{1,0:T(8,128)(2,1)}, bf16[1024,768]{1,0:T(8,128)(2,1)}, bf16[1024,768]{1,0:T(8,128)(2,1)}, bf16[1024,...) custom-call(s32[1]{0:T(128)S(6)} %copy.92.len_ref, bf16[1024,768]{1,0:T(8,128)(2,1)} %bitcast.91, ...), custom_call_target="tpu_custom_call" | custom-call | tf_op jit(solution)/shard_map/pre/pallas_call | solution.py:141
  84.7 47.4 %attention.1 = (bf16[1024,768]{1,0:T(8,128)(2,1)}, bf16[1024,768]{1,0:T(8,128)(2,1)}, bf16[1024,128]{1,0:T(8,128)(2,1)}) custom-call(s32[1]{0:T(128)S(6)} %copy.92.len_ref, bf16[1024,768]{1,0:T(8,128)(2,1)} %get-tuple-element.38.q_ref, bf16[1024,768]{1,0:T(8,128)(2,1)} %get-tuple-element.39.gm_ref, bf16[1024,128]{1,0:T(8,128)(2,1)} %get-tuple-element.40.kv_ref, ...), custom_call_target="tpu_custom_call" | custom-call | tf_op jit(solution)/shard_map/attention/pallas_call | solution.py:225
  132.1 13.8 %post.1 = (f32[1024,768]{1,0:T(8,128)}, f32[1024,768]{1,0:T(8,128)}, bf16[768,1792]{1,0:T(8,128)(2,1)}) custom-call(s32[1]{0:T(128)S(6)} %copy.92.len_ref, bf16[1024,768]{1,0:T(8,128)(2,1)} %bitcast.92, bf16[1024,768]{1,0:T(8,128)(2,1)} %bitcast.96, bf16[1024,768]{1,0:T(8,128)(2,1)} %get-tuple-element.37.ha_ref, bf16[1024,768]{1,0:T(8,128)(2,1)} %get-tuple-element.35.gy_ref, ...), custom_call_target="tpu_custom_call" | custom-call | tf_op jit(solution)/shard_map/post/pallas_call | solution.py:289
  146.0 42.6 %feed_forward.1 = (bf16[1024,768]{1,0:T(8,128)(2,1)}, f32[1024,768]{1,0:T(8,128)}, bf16[768,3072]{1,0:T(8,128)(2,1)}, bf16[768,3072]{1,0:T(8,128)(2,1)}, bf16[768,128]{1,0:T(8,128)(2,1)}) custom-call(s32[1]{0:T(128)S(6)} %copy.92.len_ref, bf16[1024,768]{1,0:T(8,128)(2,1)} %get-tuple-element.34.hm_ref, bf16[1024,768]{1,0:T(8,128)(2,1)} %get-tuple-element.35.gy_ref, ...), custom_call_target="tpu_custom_call" | custom-call | tf_op jit(solution)/shard_map/feed_forward/pallas_call | solution.py:363
  188.5 9.3 %pad_maximum_fusion = bf16[768,6272]{1,0:T(8,128)(2,1)} fusion(bf16[768,128]{1,0:T(8,128)(2,1)} %get-tuple-element.51, bf16[768,3072]{1,0:T(8,128)(2,1)} %get-tuple-element.50, bf16[768,3072]{1,0:T(8,128)(2,1)} %get-tuple-element.49), kind=kLoop, calls=%fused_computation | loop fusion | flops 28901376 | bytes 19267584 | tf_op jit(solution)/shard_map/concatenate | solution.py:462
  197.9 53.5 %reduce-scatter.5.cloned.1.call-done = bf16[24,1792]{1,0:T(8,128)(2,1)} async-done(((bf16[768,1792]{1,0:T(8,128)(2,1)}), bf16[24,1792]{1,0:T(8,128)(2,1)}) %reduce-scatter.5.cloned.1.call-update) | async-done | bytes 86032 | tf_op jit(solution)/shard_map/reduce_scatter | solution.py:460
  251.4 0.9 convert_element_type.10
  253.1 1.3 slice.64
  255.1 1.4 fusion.17
  256.5 136.2 %reduce-scatter.7.cloned.1.call-done = bf16[24,6272]{1,0:T(8,128)(2,1)} async-done(((bf16[768,6272]{1,0:T(8,128)(2,1)}), bf16[24,6272]{1,0:T(8,128)(2,1)}) %reduce-scatter.7.cloned.1.call-update) | async-done | bytes 301072
  392.7 1.1 fusion.16
  396.1 1.1 reshape.1055
  397.3 1.2 copy.83
  398.5 2.6 reshape.1056
  (80 shorter events, 7.8 us)
Async XLA Ops:
  7.2 138.8 %all-gather.2.cloned.1.call-start = ((), (), s32[]{:S(2)}) async-start(), calls=%async_computation.2 | async-start | bytes 9732096 | tf_op jit(solution)/shard_map/all_gather | solution.py:443
  10.3 2.4 copy-start.14
  10.4 2.5 copy-start.15
  10.4 2.5 copy-start.7
  10.4 2.5 copy-start.8
  10.4 2.4 copy-start.9
  10.4 2.4 copy-start.10
  10.4 2.4 copy-start.11
  10.4 2.4 copy-start.12
  10.4 2.4 copy-start.13
  10.5 2.7 copy-start.3
  10.5 2.7 copy-start.4
  10.5 2.7 copy-start.5
  12.7 238.8 %reduce-scatter.5.cloned.1.call-start = ((), (), s32[]{:S(2)}) async-start(), calls=%async_computation.3 | async-start | bytes 2838528 | tf_op jit(solution)/shard_map/reduce_scatter | solution.py:460
  13.2 8.5 %collective-permute-start = (bf16[24,1792]{1,0:T(8,128)(2,1)S(1)}, bf16[24,1792]{1,0:T(8,128)(2,1)S(1)}, u32[]{:S(2)}, u32[]{:S(2)}) collective-permute-start(bf16[24,1792]{1,0:T(8,128)(2,1)S(1)} %pad_maximum_fusion.14), channel_id=1, source_target_pairs={{0,4},{1,5},{2,6},{3,7},{4,0},{5,1},{6,2},{7,3},{8,12},{9,13},{10,... | collective-permute-start | bytes 258056 | tf_op jit(solution)/shard_map/ppermute | solution.py:396
  21.7 6.7 %collective-permute-start.1 = (bf16[48,1792]{1,0:T(8,128)(2,1)S(1)}, bf16[48,1792]{1,0:T(8,128)(2,1)S(1)}, u32[]{:S(2)}, u32[]{:S(2)}) collective-permute-start(bf16[48,1792]{1,0:T(8,128)(2,1)S(1)} %bitcast.115), channel_id=1, source_target_pairs={{0,2},{1,3},{2,0},{3,1},{4,6},{5,7},{6,4},{7,5},{8,10},{9,11},{10,... | collective-permute-start | bytes 516104 | tf_op jit(solution)/shard_map/ppermute | solution.py:396
  28.5 7.9 %collective-permute-start.2 = (bf16[96,1792]{1,0:T(8,128)(2,1)S(1)}, bf16[96,1792]{1,0:T(8,128)(2,1)S(1)}, u32[]{:S(2)}, u32[]{:S(2)}) collective-permute-start(bf16[96,1792]{1,0:T(8,128)(2,1)S(1)} %bitcast.112), channel_id=1, source_target_pairs={{0,16},{8,24},{16,0},{24,8},{1,17},{9,25},{17,1},{25,9},{2,18},{10... | collective-permute-start | bytes 1032200 | tf_op jit(solution)/shard_map/ppermute | solution.py:396
  36.6 22.5 %collective-permute-start.3 = (bf16[192,1792]{1,0:T(8,128)(2,1)S(1)}, bf16[192,1792]{1,0:T(8,128)(2,1)S(1)}, u32[]{:S(2)}, u32[]{:S(2)}) collective-permute-start(bf16[192,1792]{1,0:T(8,128)(2,1)S(1)} %bitcast.109), channel_id=1, source_target_pairs={{0,1},{1,0},{2,3},{3,2},{4,5},{5,4},{6,7},{7,6},{8,9},{9,8},{10,11... | collective-permute-start | bytes 2064392 | tf_op jit(solution)/shard_map/ppermute | solution.py:396
  60.5 10.5 %collective-permute-start.4 = (bf16[384,1792]{1,0:T(8,128)(2,1)}, bf16[384,1792]{1,0:T(8,128)(2,1)}, u32[]{:S(2)}, u32[]{:S(2)}) collective-permute-start(bf16[384,1792]{1,0:T(8,128)(2,1)} %bitcast.41), channel_id=1, source_target_pairs={{0,8},{8,0},{16,24},{24,16},{1,9},{9,1},{17,25},{25,17},{2,10},{10... | collective-permute-start | bytes 4128776 | tf_op jit(solution)/shard_map/ppermute | solution.py:396
  66.7 1.8 copy-start.1
  66.7 1.8 copy-start.2
  145.9 246.8 %reduce-scatter.7.cloned.1.call-start = ((), (), s32[]{:S(2)}) async-start(), calls=%async_computation.4 | async-start | bytes 9934848
  253.1 148.0 %copy-start.6 = (f32[24]{0:T(128)}, f32[24]{0:T(128)S(1)}, u32[]{:S(2)}) copy-start(f32[24]{0:T(128)S(1)} %get-tuple-element.115) | copy-start | bytes 292
  392.7 2.0 copy-start
Sparse Core Ops, SparseCore 0:
  12.8 92.9 all-gather.1
  146.0 105.3 reduce-scatter.4
  258.6 134.0 reduce-scatter.6

commit v2 on v1

--- a/solution.py
+++ b/solution.py
@@ -2,6 +2,7 @@
 
 import jax
 import jax.numpy as jnp
+import numpy as np
 from jax import lax
 from jax.experimental import pallas as pl
 from jax.experimental.pallas import tpu as pltpu
@@ -16,6 +17,7 @@
 ROOT_HALF = 0.7071067811865476
 INV_ROOT_TAU = 0.3989422804014327
 LANES = 128
+CHUNKS = (2,)
 BOTH = ("dp", "fsdp")
 VMEM = 60 * 1024 * 1024
 
@@ -30,23 +32,27 @@
     return pltpu.CompilerParams(vmem_limit_bytes=VMEM, **kw)
 
 
+def cost(us):
+    return pl.CostEstimate(flops=int(us * 1.0e9), bytes_accessed=int(us * 3.0e6), transcendentals=0)
+
+
 def whole(shape):
     return pl.BlockSpec(shape, lambda *_: (0,) * len(shape))
 
 
 def rotary_tables(seq_len, head_dim):
     half = ROT // 2
-    inverse_freq = 10000.0 ** (-(2.0 * jnp.arange(half, dtype=f32)) / ROT)
-    angles = jnp.arange(seq_len, dtype=f32)[:, None] * inverse_freq[None, :]
-    cos, sin = jnp.cos(angles), jnp.sin(angles)
-    one = jnp.ones((seq_len, head_dim - ROT), f32)
-    zero = jnp.zeros((seq_len, half), f32)
-    none = jnp.zeros((seq_len, head_dim - ROT), f32)
-    own = jnp.concatenate([cos, cos, one], 1)
-    up = jnp.concatenate([sin, zero, none], 1)
-    down = jnp.concatenate([zero, sin, none], 1)
-    two = lambda t: jnp.concatenate([t, t], 1)
-    return jnp.stack([two(own), two(up), two(down)])
+    inverse_freq = np.float32(10000.0) ** (-(np.float32(2.0) * np.arange(half, dtype=np.float32)) / np.float32(ROT))
+    angles = np.arange(seq_len, dtype=np.float32)[:, None] * inverse_freq[None, :]
+    cos, sin = np.cos(angles.astype(np.float64)), np.sin(angles.astype(np.float64))
+    tables = np.zeros((3, seq_len, LANES), np.float32)
+    tables[0] = 1.0
+    for at in range(0, LANES, head_dim):
+        tables[0, :, at : at + half] = cos
+        tables[0, :, at + half : at + ROT] = cos
+        tables[1, :, at : at + half] = sin
+        tables[2, :, at + half : at + ROT] = sin
+    return jnp.asarray(tables)
 
 
 def partners(v):
@@ -117,12 +123,13 @@
     hm_ref[...] = hm
     own, up, down = tab_ref[0], tab_ref[1], tab_ref[2]
     scale = (kv_width // 2) ** -0.5
+    lin = dot(ha, w_ref[:, :c_out], 1, 0)
+    query = lin[:, :width] + vec[QB : QB + 1]
     for p in range(width // LANES):
         cols = slice(p * LANES, (p + 1) * LANES)
-        lin = dot(ha, w_ref[:, cols], 1, 0) + vec[QB : QB + 1, cols]
-        rot = rotate(lin, own, up, down).astype(bf16)
+        rot = rotate(query[:, cols], own, up, down).astype(bf16)
         q_ref[:, cols] = (rot.astype(f32) * scale).astype(bf16)
-    lin = dot(ha, w_ref[:, width:c_out], 1, 0) + vec[16 + KB : 17 + KB, :kv_width]
+    lin = lin[:, width:] + vec[16 + KB : 17 + KB, :kv_width]
     lane = lax.broadcasted_iota(jnp.int32, (rows, kv_width), 1)
     kv_ref[...] = jnp.where(lane < kv_width // 2, rotate(lin, own, up, down), lin).astype(bf16)
     keep = kept_rows(i, rows, len_ref[0])
@@ -157,6 +164,7 @@
             jax.ShapeDtypeStruct((32, width), f32),
         ],
         compiler_params=params(),
+        cost_estimate=cost(9),
         name="pre",
     )(length, x, cot, w1, tables)
 
@@ -233,11 +241,23 @@
         ),
         out_shape=[wide, wide, jax.ShapeDtypeStruct((tokens, kv_width), bf16)],
         compiler_params=params(),
+        cost_estimate=cost(47),
         name="attention",
     )(length, q, gm, kv, tables)
 
 
-def post_kernel(len_ref, x_ref, cot_ref, ha_ref, gy_ref, mix_ref, dq_ref, dkv_ref, w_ref, vec_ref, out_ref, gt_ref, dw_ref, acc, sums, *, dims):
+def split_halves(send_ref, keep_ref, low_s, cols, at, core, half):
+    for g in range(low_s.shape[0] // (2 * half)):
+        to, base = pl.ds(g * half, half), g * 2 * half
+        send_ref[to, at] = low_s[pl.ds(pl.multiple_of(base + (1 - core) * half, half), half), :cols]
+        keep_ref[to, at] = low_s[pl.ds(pl.multiple_of(base + core * half, half), half), :cols]
+
+
+def row_sum(v):
+    return jnp.sum(v, axis=1, keepdims=True)
+
+
+def grads_kernel(info, ha_ref, gy_ref, mix_ref, dq_ref, dkv_ref, w_ref, send_ref, keep_ref, acc, sums, low_s, *, dims, half):
     width, kv_width, rows, per_row, per_kv = dims
     i = pl.program_id(0)
     c_out = width + kv_width
@@ -248,143 +268,232 @@
         acc[...] = jnp.zeros_like(acc)
         sums[...] = jnp.zeros_like(sums)
 
-    keep = kept_rows(i, rows, len_ref[0])
-    vec = vec_ref[...]
-    x = x_ref[...].astype(f32)
-    mixed, gy, ha, dq, dkv = mix_ref[...], gy_ref[...], ha_ref[...], dq_ref[...], dkv_ref[...]
-    attn_out = dot(mixed, w_ref[:, c_out:c_vec], 1, 0) + vec[OB : OB + 1]
-    out_ref[...] = x + keep * attn_out
+    gy, ha, dq, dkv = gy_ref[...], ha_ref[...], dq_ref[...], dkv_ref[...]
     acc[:, :width] += dot(ha, dq, 0, 0)
     acc[:, width:c_out] += dot(ha, dkv, 0, 0)
-    acc[:, c_out:c_vec] += dot(mixed, gy, 0, 0)
-    grad = dot(dq, w_ref[:, :width], 1, 1) + dot(dkv, w_ref[:, width:c_out], 1, 1)
-    normed, scaled = standardise(x)
-    gt_ref[...] = cot_ref[...].astype(f32) + norm_back(grad, normed, scaled, vec[GA : GA + 1])
+    acc[:, c_out:c_vec] += dot(mix_ref[...], gy, 0, 0)
     sums[QB : QB + 1] += col_sum(dq.astype(f32))
     sums[OB : OB + 1] += col_sum(gy.astype(f32))
-    sums[GA : GA + 1] += col_sum(grad * normed)
-    sums[BA : BA + 1] += col_sum(grad)
     sums[8:9, :kv_width] += col_sum(dkv.astype(f32))
 
     @pl.when(i == pl.num_programs(0) - 1)
     def _():
-        dw_ref[:, :c_vec] = acc[...].astype(bf16)
+        w_q, w_kv = w_ref[:, :width].astype(f32), w_ref[:, width:c_out].astype(f32)
+        shift = row_sum(w_q * sums[QB : QB + 1]) + row_sum(w_kv * sums[8:9, :kv_width])
+        inner = row_sum(w_q * acc[:, :width]) + row_sum(w_kv * acc[:, width:c_out])
+        vec = w_ref[:, c_vec:].astype(f32)
+        gain = (inner - vec[:, BA : BA + 1] * shift) / vec[:, GA : GA + 1]
+        low_s[:, :c_vec] = acc[...].astype(bf16)
         spread = spread_key_bias(width, kv_width, per_row, per_kv)
         low = sums[...].astype(bf16)
         key = dot(low[8:16, :kv_width], spread, 1, 1)
         row = lax.broadcasted_iota(jnp.int32, (16, width), 0)
         both = jnp.where(row == 8, jnp.concatenate([key, key], 0), low.astype(f32))
-        both = jnp.concatenate([both, jnp.zeros((LANES - 16, width), f32)], 0)
-        dw_ref[:, c_vec:] = both.T.astype(bf16)
-
-
-def post(length, x, cot, ha, gy, mixed, dq, dkv, w1, vec, shards):
-    tokens, width = x.shape
+        both = jnp.concatenate([both, jnp.zeros((LANES - 16, width), f32)], 0).T
+        lane = lax.broadcasted_iota(jnp.int32, (width, LANES), 1)
+        both = jnp.where(lane == GA, gain, jnp.where(lane == BA, shift, both))
+        low_s[:, c_vec:] = both.astype(bf16)
+        split_halves(send_ref, keep_ref, low_s, c_vec + LANES, slice(None), info[1], half)
+
+
+def attention_grads(info, ha, gy, mixed, dq, dkv, w1, shards, half):
+    tokens, width = ha.shape
     kv_width = dkv.shape[1]
     rows = 256
     blk = pl.BlockSpec((rows, width), lambda i, *_: (i, 0))
     kvb = pl.BlockSpec((rows, kv_width), lambda i, *_: (i, 0))
     dims = (width, kv_width, rows, width // shards, kv_width // shards)
-    full = jax.ShapeDtypeStruct((tokens, width), f32)
+    cut = (width // 2, w1.shape[1])
     return pl.pallas_call(
-        functools.partial(post_kernel, dims=dims),
+        functools.partial(grads_kernel, dims=dims, half=half),
         grid_spec=pltpu.PrefetchScalarGridSpec(
             num_scalar_prefetch=1,
             grid=(tokens // rows,),
-            in_specs=[blk, blk, blk, blk, blk, blk, kvb, whole(w1.shape), whole(vec.shape)],
-            out_specs=[blk, blk, whole(w1.shape)],
-            scratch_shapes=[pltpu.VMEM((width, w1.shape[1] - LANES), f32), pltpu.VMEM((16, width), f32)],
+            in_specs=[blk, blk, blk, blk, kvb, whole(w1.shape)],
+            out_specs=[whole(cut), whole(cut)],
+            scratch_shapes=[
+                pltpu.VMEM((width, w1.shape[1] - LANES), f32),
+                pltpu.VMEM((16, width), f32),
+                pltpu.VMEM(w1.shape, bf16),
+            ],
         ),
-        out_shape=[full, full, jax.ShapeDtypeStruct(w1.shape, bf16)],
+        out_shape=[jax.ShapeDtypeStruct(cut, bf16)] * 2,
         compiler_params=params(),
-        name="post",
-    )(length, x, cot, ha, gy, mixed, dq, dkv, w1, vec)
-
-
-def ff_kernel(len_ref, hm_ref, gy_ref, wu_ref, wd_ref, vec_ref, x_ref, base_ref, gt_ref, out_ref, gtok_ref, dwu_ref, dwd_ref, dv_ref, act_s, gup_s, mlp, gh, sums, *, rows):
+        cost_estimate=cost(8),
+        name="attention_grads",
+    )(info, ha, gy, mixed, dq, dkv, w1)
+
+
+SHIFT, INNER = 8, 9
+
+
+def ff_kernel(*refs, rows, chunk, first, final, half):
+    refs = list(refs)
+    take = lambda k: [refs.pop(0) for _ in range(k)]
+    info, hm_ref, gy_ref, wu_ref, wd_ref, vec_ref = take(6)
+    (col_in,) = (None,) if first else take(1)
+    (vcol_ref,) = take(1) if final else (None,)
+    act_ref, gup_ref = take(2)
+    (col_out,) = (None,) if final else take(1)
+    send_ref, keep_ref, cols, low_s = refs
     j = pl.program_id(0)
     tokens, width = hm_ref.shape
-    blocks = tokens // rows
 
     @pl.when(j == 0)
     def _():
-        mlp[...] = jnp.zeros_like(mlp)
-        gh[...] = jnp.zeros_like(gh)
-        sums[...] = jnp.zeros_like(sums)
-
-    bias = vec_ref[pl.ds(UB + j, 1), :]
-    total = jnp.zeros((1, wu_ref.shape[1]), f32)
-    for i in range(blocks):
+        cols[...] = jnp.zeros_like(cols) if first else col_in[...]
+
+    bias = vec_ref[pl.ds(UB + chunk + j, 1), :]
+    total = jnp.zeros((1, width), f32)
+    for i in range(tokens // rows):
         r = pl.ds(i * rows, rows)
         u = dot(hm_ref[r, :], wu_ref[...], 1, 0) + bias
         cdf = 0.5 * (1.0 + lax.erf(u * ROOT_HALF))
         pdf = jnp.exp(-0.5 * u * u) * INV_ROOT_TAU
-        act = (u * cdf).astype(bf16)
-        act_s[r, :] = act
+        act_ref[r, :] = (u * cdf).astype(bf16)
         grad = (dot(gy_ref[r, :], wd_ref[...], 1, 1) * (cdf + u * pdf)).astype(bf16)
-        gup_s[r, :] = grad
+        gup_ref[r, :] = grad
         total = total + col_sum(grad.astype(f32))
-        mlp[r, :] += dot(act, wd_ref[...], 1, 0)
-        gh[r, :] += dot(grad, wu_ref[...], 1, 1)
-    sums[pl.ds(j, 1), :] = total
-    dwd_ref[...] = dot(act_s[...], gy_ref[...], 0, 0).astype(bf16)
-    dwu_ref[...] = dot(hm_ref[...], gup_s[...], 0, 0).astype(bf16)
+    at = pl.multiple_of(j * 2 * width, LANES)
+    d_up = dot(hm_ref[...], gup_ref[...], 0, 0)
+    low_s[...] = d_up.astype(bf16)
+    w_up = wu_ref[...].astype(f32)
+    lane = lax.broadcasted_iota(jnp.int32, (width, LANES), 1)
+    mine = jnp.where(lane == chunk + j, jnp.broadcast_to(total, (LANES, width)).T, 0.0)
+    mine = jnp.where(lane == SHIFT, row_sum(w_up * total), mine)
+    cols[...] += jnp.where(lane == INNER, row_sum(w_up * d_up), mine)
+    split_halves(send_ref, keep_ref, low_s, width, pl.ds(at, width), info[1], half)
+    low_s[...] = dot(act_ref[...], gy_ref[...], 0, 0).astype(bf16)
+    at = pl.multiple_of(at + width, LANES)
+    split_halves(send_ref, keep_ref, low_s, width, pl.ds(at, width), info[1], half)
 
     @pl.when(j == pl.num_programs(0) - 1)
     def _():
-        gain = vec_ref[GM : GM + 1]
-        down_bias = vec_ref[DB : DB + 1]
-        d_gain = jnp.zeros((1, width), f32)
-        d_shift = jnp.zeros((1, width), f32)
-        for i in range(blocks):
-            r = pl.ds(i * rows, rows)
-            keep = kept_rows(i, rows, len_ref[0])
-            out_ref[r, :] = (base_ref[r, :] + keep * (mlp[r, :] + down_bias)).astype(bf16)
-            normed, scaled = standardise(x_ref[r, :].astype(f32))
-            grad = gh[r, :]
-            gtok_ref[r, :] = gt_ref[r, :] + norm_back(grad, normed, scaled, gain)
-            d_gain = d_gain + col_sum(grad * normed)
-            d_shift = d_shift + col_sum(grad)
-        blocks_up = pl.num_programs(0)
-        sums[4:5, :] = d_gain
-        sums[5:6, :] = d_shift
-        both = jnp.concatenate([sums[...], jnp.zeros((LANES - 8, width), f32)], 0)
-        dv_ref[...] = both.T.astype(bf16)
-
-
-def feed_forward(length, hm, gy, w2, vec, x, base, gt):
-    tokens, width = x.shape
+        if not final:
+            col_out[...] = cols[...]
+            return
+        vec = vcol_ref[...].astype(f32)
+        now = cols[...]
+        gain = (now[:, INNER : INNER + 1] - vec[:, BM : BM + 1] * now[:, SHIFT : SHIFT + 1]) / vec[:, GM : GM + 1]
+        low_s[:, :LANES] = jnp.where(lane == INNER, gain, now).astype(bf16)
+        at = pl.ds(send_ref.shape[1] - LANES, LANES)
+        split_halves(send_ref, keep_ref, low_s, LANES, at, info[1], half)
+
+
+def feed_forward(info, hm, gy, w2, vec, w1, state, chunk, count, half):
+    tokens, width = hm.shape
     blocks = w2.shape[1] // (2 * width)
+    tok = (tokens, width)
+    first, final = state is None, chunk + count == blocks
     one = lambda s: pl.BlockSpec(s, lambda *_: (0, 0), pipeline_mode=pl.Buffered(1))
-    up = pl.BlockSpec((width, width), lambda j, *_: (0, j))
-    dn = pl.BlockSpec((width, width), lambda j, *_: (0, j + blocks))
-    tok = (tokens, width)
-    half = jax.ShapeDtypeStruct((width, blocks * width), bf16)
-    return pl.pallas_call(
-        functools.partial(ff_kernel, rows=256),
+    col = pl.BlockSpec(tok, lambda j, *_: (0, j))
+    up = pl.BlockSpec((width, width), lambda j, *_: (0, j + chunk))
+    dn = pl.BlockSpec((width, width), lambda j, *_: (0, j + chunk + blocks))
+    args = [hm, gy, w2, w2, vec]
+    specs = [one(tok), one(tok), up, dn, one(vec.shape)]
+    last = w1.shape[1] // LANES - 1
+    if not first:
+        args += [state]
+        specs += [one((width, LANES))]
+    if final:
+        args += [w1]
+        specs += [pl.BlockSpec((width, LANES), lambda *_: (0, last), pipeline_mode=pl.Buffered(1))]
+    long = jax.ShapeDtypeStruct((tokens, count * width), bf16)
+    shapes, outs = [long, long], [col, col]
+    if not final:
+        shapes += [jax.ShapeDtypeStruct((width, LANES), f32)]
+        outs += [one((width, LANES))]
+    cut = (width // 2, count * 2 * width + (LANES if final else 0))
+    shapes += [jax.ShapeDtypeStruct(cut, bf16)] * 2
+    outs += [one(cut)] * 2
+    got = pl.pallas_call(
+        functools.partial(ff_kernel, rows=256, chunk=chunk, first=first, final=final, half=half),
         grid_spec=pltpu.PrefetchScalarGridSpec(
             num_scalar_prefetch=1,
-            grid=(blocks,),
-            in_specs=[one(tok), one(tok), up, dn, one(vec.shape), one(tok), one(tok), one(tok)],
-            out_specs=[whole(tok), whole(tok), up, up, whole((width, LANES))],
-            scratch_shapes=[
-                pltpu.VMEM((tokens, width), bf16),
-                pltpu.VMEM((tokens, width), bf16),
-                pltpu.VMEM(tok, f32),
-                pltpu.VMEM(tok, f32),
-                pltpu.VMEM((8, width), f32),
-            ],
+            grid=(count,),
+            in_specs=specs,
+            out_specs=outs,
+            scratch_shapes=[pltpu.VMEM((width, LANES), f32), pltpu.VMEM((width, width), bf16)],
         ),
-        out_shape=[
-            jax.ShapeDtypeStruct(tok, bf16),
-            jax.ShapeDtypeStruct(tok, f32),
-            half,
-            half,
-            jax.ShapeDtypeStruct((width, LANES), bf16),
-        ],
+        out_shape=shapes,
         compiler_params=params(),
+        cost_estimate=cost(7 * count),
         name="feed_forward",
-    )(length, hm, gy, w2, w2, vec, x, base, gt)
+    )(info, *args)
+    act, gup = got[:2]
+    return act, gup, None if final else got[2], got[-2], got[-1]
+
+
+def out_kernel(*refs, pieces, c_out, rows):
+    info, x_ref, mix_ref, w1_ref, wd_ref, vec_ref = refs[:6]
+    acts, out_ref = refs[6:-1], refs[-1]
+    width = x_ref.shape[1]
+    total = dot(mix_ref[...], w1_ref[:, c_out : c_out + width], 1, 0) + vec_ref[OB : OB + 1] + vec_ref[DB : DB + 1]
+    at = 0
+    for act_ref, count in zip(acts, pieces):
+        for k in range(count):
+            act = act_ref[:, k * width : (k + 1) * width]
+            total = total + dot(act, wd_ref[:, at : at + width], 1, 0)
+            at += width
+    keep = kept_rows(pl.program_id(0), rows, info[0])
+    out_ref[...] = (x_ref[...].astype(f32) + keep * total).astype(bf16)
+
+
+def layer_output(info, x, mixed, w1, w2, vec, acts, c_out):
+    tokens, width = x.shape
+    rows = 256
+    half = w2.shape[1] // 2
+    blk = lambda n: pl.BlockSpec((rows, n), lambda i, *_: (i, 0))
+    one = lambda s, *at: pl.BlockSpec(s, lambda *_: at, pipeline_mode=pl.Buffered(1))
+    return pl.pallas_call(
+        functools.partial(out_kernel, pieces=[a.shape[1] // width for a in acts], c_out=c_out, rows=rows),
+        grid_spec=pltpu.PrefetchScalarGridSpec(
+            num_scalar_prefetch=1,
+            grid=(tokens // rows,),
+            in_specs=[blk(width), blk(width), one(w1.shape, 0, 0), one((width, half), 0, 1), one(vec.shape, 0, 0)]
+            + [blk(a.shape[1]) for a in acts],
+            out_specs=blk(width),
+        ),
+        out_shape=jax.ShapeDtypeStruct((tokens, width), bf16),
+        compiler_params=params(),
+        cost_estimate=cost(9),
+        name="layer_output",
+    )(info, x, mixed, w1, w2, vec, *acts)
+
+
+def token_kernel(*refs, pieces, kv_width):
+    x_ref, cot_ref, dq_ref, dkv_ref, w1_ref, wu_ref, vec_ref = refs[:7]
+    gups, out_ref = refs[7:-1], refs[-1]
+    width = x_ref.shape[1]
+    normed, scaled = standardise(x_ref[...].astype(f32))
+    grad = dot(dq_ref[...], w1_ref[:, :width], 1, 1) + dot(dkv_ref[...], w1_ref[:, width : width + kv_width], 1, 1)
+    total = norm_back(grad, normed, scaled, vec_ref[GA : GA + 1])
+    at, grad = 0, None
+    for gup_ref, count in zip(gups, pieces):
+        part = dot(gup_ref[...], wu_ref[:, at : at + count * width], 1, 1)
+        grad = part if grad is None else grad + part
+        at += count * width
+    total = total + norm_back(grad, normed, scaled, vec_ref[GM : GM + 1])
+    out_ref[...] = cot_ref[...].astype(f32) + total
+
+
+def token_grads(x, cot, dq, dkv, w1, w2, vec, gups):
+    tokens, width = x.shape
+    rows = 256
+    half = w2.shape[1] // 2
+    blk = lambda n: pl.BlockSpec((rows, n), lambda i: (i, 0))
+    one = lambda s: pl.BlockSpec(s, lambda *_: (0, 0), pipeline_mode=pl.Buffered(1))
+    return pl.pallas_call(
+        functools.partial(token_kernel, pieces=[g.shape[1] // width for g in gups], kv_width=dkv.shape[1]),
+        grid=(tokens // rows,),
+        in_specs=[blk(width), blk(width), blk(width), blk(dkv.shape[1]), one(w1.shape), one((width, half)), one(vec.shape)]
+        + [blk(g.shape[1]) for g in gups],
+        out_specs=blk(width),
+        out_shape=jax.ShapeDtypeStruct((tokens, width), f32),
+        compiler_params=params(),
+        cost_estimate=cost(11),
+        name="token_grads",
+    )(x, cot, dq, dkv, w1, w2, vec, *gups)
 
 
 def bits_of(axis, size):
@@ -407,6 +516,71 @@
         high = jnp.where(here == 0, got, cur)
         cur = jnp.concatenate([low, high], where)
     return cur.reshape(-1, cols)
+
+
+def add(a, b):
+    return (a.astype(f32) + b.astype(f32)).astype(bf16)
+
+
+def tie(*values):
+    return lax.optimization_barrier(values)
+
+
+class Scatter:
+    def __init__(self, send, keep, orders, tail, index_order):
+        self.index_order = index_order
+        self.cols = send.shape[1]
+        dims = [1 if b == ("dp", 0) else 2 for b in index_order]
+        self.shape = (*dims, send.shape[0] >> (len(index_order) - 1), self.cols)
+        self.steps = [[("dp", 0)]] + [list(s) for s in zip(*orders)] + [[b] for b in tail]
+        self.pending = [(send, keep.reshape(self.shape))]
+        self.flying = None
+        self.result = None
+
+    def ready(self):
+        return [send for send, _ in self.pending]
+
+    def start(self):
+        bits = self.steps.pop(0)
+        self.flying = [(swap(send, *bit), keep) for (send, keep), bit in zip(self.pending, bits)]
+
+    def arrived(self):
+        return [got for got, _ in self.flying]
+
+    def finish(self, arrived):
+        parts = [add(keep, got.reshape(keep.shape)) for got, (_, keep) in zip(arrived, self.flying)]
+        if not self.steps:
+            (part,) = parts
+            self.result = part.reshape(-1, self.cols)
+            return
+        bits = self.steps[0]
+        if len(parts) > len(bits):
+            parts = [jnp.concatenate(parts, -1)]
+        if len(parts) < len(bits):
+            (part,) = parts
+            step = self.cols // LANES // len(bits) * LANES
+            edges = [k * step for k in range(len(bits))] + [self.cols]
+            parts = [part[..., lo:hi] for lo, hi in zip(edges, edges[1:])]
+        self.pending = []
+        for part, (axis, bit) in zip(parts, bits):
+            here, where = (lax.axis_index(axis) >> bit) & 1, self.index_order.index((axis, bit))
+            send = lax.dynamic_slice_in_dim(part, 1 - here, 1, where)
+            keep = lax.dynamic_slice_in_dim(part, here, 1, where)
+            self.pending.append((send.reshape(-1, part.shape[-1]), keep))
+
+
+def beside(streams, work, *inputs):
+    streams = [s for s in streams if s.result is None]
+    ready = [s.ready() for s in streams]
+    ready, inputs = tie(ready, inputs)
+    for stream, sends in zip(streams, ready):
+        stream.pending = [(send, keep) for send, (_, keep) in zip(sends, stream.pending)]
+        stream.start()
+    out = work(*inputs)
+    arrived, out = tie([s.arrived() for s in streams], out)
+    for stream, a in zip(streams, arrived):
+        stream.finish(a)
+    return out
 
 
 def body(
@@ -456,18 +630,45 @@
     tables = rotary_tables(seq_len, kv_width // 2)
     q, kv, ha, hm, gy, gm, vec = pre(lengths, x, cot, w1, tables, kv_width, shards)
     mixed, dq, dkv = attention(lengths, q, gm, kv, tables)
-    base, gt, dw1 = post(lengths, x, cot, ha, gy, mixed, dq, dkv, w1, vec, shards)
-    own1 = lax.psum_scatter(dw1, BOTH, scatter_dimension=0, tiled=True)
-    layer_out, gtok, dwu, dwd, dv = feed_forward(lengths, hm, gy, w2, vec, x, base, gt)
-    own2 = lax.psum_scatter(jnp.concatenate([dwu, dwd, dv], 1), BOTH, scatter_dimension=0, tiled=True)
-
-    own1, own2 = own1.astype(f32), own2.astype(f32)
+    half = rows * n_fsdp
+    core = lax.axis_index("dp") & 1
+    info = jnp.concatenate([lengths, core[None].astype(jnp.int32)])
+    x_bits, y_bits, z_bits = fs_bits[:1], dp_bits[1:], fs_bits[1:]
+    send, keep = attention_grads(info, ha, gy, mixed, dq, dkv, w1, shards, half)
+    attn = Scatter(send, keep, [z_bits], x_bits + y_bits, index_order)
+    xy = [x_bits + y_bits, y_bits + x_bits]
+
+    hm, gy = beside([attn], lambda *v: v, hm, gy)
+    n0 = CHUNKS[0]
+    act0, gup0, state, send, keep = beside(
+        [attn], lambda hm, gy: feed_forward(info, hm, gy, w2, vec, w1, None, 0, n0, half), hm, gy
+    )
+    ff0 = Scatter(send, keep, xy, z_bits, index_order)
+    n1 = blocks - n0
+    act1, gup1, _, send, keep = beside(
+        [attn, ff0], lambda hm, gy, state: feed_forward(info, hm, gy, w2, vec, w1, state, n0, n1, half), hm, gy, state
+    )
+    ff1 = Scatter(send, keep, xy, z_bits, index_order)
+    layer_out = beside(
+        [ff1, ff0, attn], lambda x, *acts: layer_output(info, x, mixed, w1, w2, vec, acts, width + kv_width), x, act0, act1
+    )
+    gtok = beside(
+        [ff0, ff1, attn], lambda cot, *gups: token_grads(x, cot, dq, dkv, w1, w2, vec, gups), cot, gup0, gup1
+    )
+    while any(s.result is None for s in (attn, ff0, ff1)):
+        beside([ff0, ff1, attn], lambda *v: v)
+    own1, own_a, own_b = attn.result, ff0.result, ff1.result
+    own_v = own_b[:, -LANES:]
+    pieces = [own_a.reshape(rows, n0, 2, width), own_b[:, : n1 * 2 * width].reshape(rows, n1, 2, width)]
+    pieces = jnp.concatenate(pieces, 1).astype(f32)
+
+    own1 = own1.astype(f32)
     c_out = width + kv_width
     c_vec = c_out + width
     v1 = own1[:, c_vec:].T
-    v2 = own2[:, 2 * ff :].T
-    g_up = own2[:, :ff].reshape(rows, blocks, shards, rows).transpose(0, 2, 1, 3).reshape(rows, ff)
-    g_dn = own2[:, ff : 2 * ff].reshape(rows, blocks, width).transpose(1, 0, 2).reshape(blocks * rows, width)
+    v2 = own_v.astype(f32).T
+    g_up = pieces[:, :, 0].reshape(rows, blocks, shards, rows).transpose(0, 2, 1, 3).reshape(rows, ff)
+    g_dn = pieces[:, :, 1].transpose(1, 0, 2).reshape(blocks * rows, width)
     return (
         layer_out.reshape(tokens.shape),
         gtok.reshape(tokens.shape),
@@ -479,8 +680,8 @@
         v1[OB],
         v1[GA],
         v1[BA],
-        v2[4],
-        v2[5],
+        v2[INNER],
+        v2[SHIFT],
         g_up,
         v2[:4].reshape(-1),
         g_dn,

time: 409 us -> 291 us (0.71)
  waiting for transfers between devices: 226 us -> 64.4 us
  starting transfers between devices: 9.13 us -> 34.7 us
  Pallas kernels: 114 us -> 130 us
    unnamed x4 -> x1, waiting for transfers between devices: 136 us -> 0.02 us
    reduce_scatter x1 -> x0, waiting for transfers between devices: 53.5 us -> none  [body(): own1 = lax.psum_scatter(dw1, BOTH, scatter_dimension=0, tiled=True)]
    ppermute x5 -> x24, waiting for transfers between devices: 36.4 us -> 64.4 us  [swap(): return lax.ppermute(v, axis, [(i, i ^ 1 << bit) for i in range(size)])]
    ppermute x5 -> x24, starting transfers between devices: 9.01 us -> 34.6 us  [swap(): return lax.ppermute(v, axis, [(i, i ^ 1 << bit) for i in range(size)])]
    pallas_call x2 -> x5, Pallas kernels: 56.4 us -> 73.6 us  [the longest x2 36.1 us: feed_forward(): pl.pallas_call(functools.partial(ff_kernel, rows=256, chunk=chunk, first=...]
    convert_element_type x2 -> x18, other arithmetic: 0.94 us -> 13.7 us  [the longest x16 13.4 us: add(): return (a.astype(f32) + b.astype(f32)).astype(bf16)]
    concatenate x1 -> x3, other arithmetic: 9.32 us -> 0.65 us  [the longest x1 0.59 us: body(): info = jnp.concatenate([lengths, core[None].astype(jnp.int32)])]
    concatenate x3 -> x0, local copies, waits for them, and re-layouts: 5.23 us -> none  [rotary_tables(): two = lambda t: jnp.concatenate([t, t], 1)]
  transfers between devices with their start and end apart: 8 -> 25, of which waited for: 6 -> 14; matrix products, arithmetic and copies ran while one was open for 7% -> 4% of each run, Pallas kernels for 28% -> 45%
where the time goes in v2:
time: 291 us; the launch traced here: 288 us
  Pallas kernels  130 us (45%)
  waiting for transfers between devices  64.4 us (22%)
  starting transfers between devices  34.7 us (12%)
  local copies, waits for them, and re-layouts  26.7 us (9%)
  other arithmetic  16.4 us (6%)
  between operations  15.6 us (5%)
    ppermute x24, waiting for transfers between devices, swap(): return lax.ppermute(v, axis, [(i, i ^ 1 << bit) for i in range(size)])  64.4 us
    pallas_call x1, Pallas kernels, attention(): pl.pallas_call(functools.partial(attn_kernel, qb=256), grid_spec=pltpu.Pr...  47.2 us
    pallas_call x2, Pallas kernels, feed_forward(): pl.pallas_call(functools.partial(ff_kernel, rows=256, chunk=chunk, first=...  36.1 us
    ppermute x24, starting transfers between devices, swap(): return lax.ppermute(v, axis, [(i, i ^ 1 << bit) for i in range(size)])  34.6 us
    pallas_call x1, Pallas kernels, token_grads(): pl.pallas_call(functools.partial(token_kernel, pieces=[g.shape[1] // widt...  14.1 us
    convert_element_type x16, other arithmetic, add(): return (a.astype(f32) + b.astype(f32)).astype(bf16)  13.4 us
    pallas_call x1, Pallas kernels, layer_output(): pl.pallas_call(functools.partial(out_kernel, pieces=[a.shape[1] // width...  12.5 us
    pallas_call x1, Pallas kernels, attention_grads(): pl.pallas_call(functools.partial(grads_kernel, dims=dims, half=half), gri...  11 us
  transfers between devices with their start and end apart: 25, of which 14 were waited for; matrix products, arithmetic and copies ran while one was open for 4% of the time, Pallas kernels for 45%

profile of v2, /device:TPU:0, one launch (start us, length us, event | category | flops | bytes accessed | tf_op | source)
XLA Modules:
  0.0 287.7 jit_solution(5725516520892762744)
XLA Ops:
  8.2 2.1 reshape.1412
  13.6 4.1 %collective-permute-start = (bf16[24,1792]{1,0:T(8,128)(2,1)S(1)}, bf16[24,1792]{1,0:T(8,128)(2,1)S(1)}, u32[]{:S(2)}, u32[]{:S(2)}) collective-permute-start(bf16[24,1792]{1,0:T(8,128)(2,1)S(1)} %pad_maximum_fusion.12), channel_id=1, source_target_pairs={{0,4},{1,5},{2,6},{3,7},{4,0},{5,1},{6,2},{7,3},{8,12},{9,13},{10,... | collective-permute-start | bytes 258056 | tf_op jit(solution)/shard_map/ppermute | solution.py:505
  17.7 4.4 %collective-permute-done = bf16[24,1792]{1,0:T(8,128)(2,1)S(1)} collective-permute-done((bf16[24,1792]{1,0:T(8,128)(2,1)S(1)}, bf16[24,1792]{1,0:T(8,128)(2,1)S(1)}, u32[]{:S(2)}, u32[]{:S(2)}) %collective-permute-start) | collective-permute-done | bytes 86048 | tf_op jit(solution)/shard_map/ppermute | solution.py:505
  23.0 6.8 %collective-permute-done.1 = bf16[48,1792]{1,0:T(8,128)(2,1)S(1)} collective-permute-done((bf16[48,1792]{1,0:T(8,128)(2,1)S(1)}, bf16[48,1792]{1,0:T(8,128)(2,1)S(1)}, u32[]{:S(2)}, u32[]{:S(2)}) %collective-permute-start.1) | collective-permute-done | bytes 172064 | tf_op jit(solution)/shard_map/ppermute | solution.py:505
  31.6 5.5 %collective-permute-done.2 = bf16[96,1792]{1,0:T(8,128)(2,1)S(1)} collective-permute-done((bf16[96,1792]{1,0:T(8,128)(2,1)S(1)}, bf16[96,1792]{1,0:T(8,128)(2,1)S(1)}, u32[]{:S(2)}, u32[]{:S(2)}) %collective-permute-start.2) | collective-permute-done | bytes 344096 | tf_op jit(solution)/shard_map/ppermute | solution.py:505
  39.1 20.1 %collective-permute-done.3 = bf16[192,1792]{1,0:T(8,128)(2,1)S(1)} collective-permute-done((bf16[192,1792]{1,0:T(8,128)(2,1)S(1)}, bf16[192,1792]{1,0:T(8,128)(2,1)S(1)}, u32[]{:S(2)}, u32[]{:S(2)}) %collective-permute-start.3) | collective-permute-done | bytes 688160 | tf_op jit(solution)/shard_map/ppermute | solution.py:505
  62.1 1.9 collective-permute-done.4
  64.5 1.8 copy.120
  66.3 9.1 %pre.1 = (bf16[1024,768]{1,0:T(8,128)(2,1)}, bf16[1024,128]{1,0:T(8,128)(2,1)}, bf16[1024,768]{1,0:T(8,128)(2,1)}, bf16[1024,768]{1,0:T(8,128)(2,1)}, bf16[1024,...) custom-call(s32[1]{0:T(128)S(6)} %copy.148.len_ref, bf16[1024,768]{1,0:T(8,128)(2,1)} %bitcast.235, ...), custom_call_target="tpu_custom_call" | custom-call | flops 8999999488 | bytes 27000000 | tf_op jit(solution)/shard_map/pre/pallas_call | solution.py:148
  75.4 47.2 %attention.1 = (bf16[1024,768]{1,0:T(8,128)(2,1)}, bf16[1024,768]{1,0:T(8,128)(2,1)}, bf16[1024,128]{1,0:T(8,128)(2,1)}) custom-call(s32[1]{0:T(128)S(6)} %copy.148.len_ref, bf16[1024,768]{1,0:T(8,128)(2,1)} %get-tuple-element.101.q_ref, bf16[1024,768]{1,0:T(8,128)(2,1)} %get-tuple-element.102.gm_ref, bf16[1024,128]{1,0:T(8,128)(2,1)} %get-tuple-element.103.kv_ref, ...), custom_call_target="tpu_custom_call" | custom-call | flops 46999998464 | bytes 141000000 | tf_op jit(solution)/shard_map/attention/pallas_call | solution.py:233
  122.6 11.0 %attention_grads.1 = (bf16[384,1792]{1,0:T(8,128)(2,1)}, bf16[384,1792]{1,0:T(8,128)(2,1)}) custom-call(s32[2]{0:T(128)} %pad_add_fusion.info.refs_0_, bf16[1024,768]{1,0:T(8,128)(2,1)} %get-tuple-element.99.ha_ref, bf16[1024,768]{1,0:T(8,128)(2,1)} %get-tuple-element.131.gy_ref.refs_2_, bf16[1024,768]{1,0:T(8,128)(2,1)} %get-tuple-element.104.mix_ref.refs_2_, ...), custom_call_target="tpu_custom_call" | custom-call | flops 8000000000 | bytes 24000000 | tf_op jit(solution)/shard_map/attention_grads/pallas_call | solution.py:307
  133.7 3.2 %collective-permute-done.5 = bf16[384,1792]{1,0:T(8,128)(2,1)S(1)} collective-permute-done((bf16[384,1792]{1,0:T(8,128)(2,1)}, bf16[384,1792]{1,0:T(8,128)(2,1)S(1)}, u32[]{:S(2)}, u32[]{:S(2)}) %collective-permute-start.5) | collective-permute-done | bytes 1376288 | tf_op jit(solution)/shard_map/ppermute | solution.py:505
  138.6 3.1 %collective-permute-start.6 = (bf16[192,1792]{1,0:T(8,128)(2,1)S(1)}, bf16[192,1792]{1,0:T(8,128)(2,1)S(1)}, u32[]{:S(2)}, u32[]{:S(2)}) collective-permute-start(bf16[192,1792]{1,0:T(8,128)(2,1)S(1)} %bitcast.205), channel_id=1, source_target_pairs={{0,2},{1,3},{2,0},{3,1},{4,6},{5,7},{6,4},{7,5},{8,10},{9,11},{10,... | collective-permute-start | bytes 2064392 | tf_op jit(solution)/shard_map/ppermute | solution.py:505
  141.7 17.7 %feed_forward.2 = (bf16[1024,1536]{1,0:T(8,128)(2,1)}, bf16[1024,1536]{1,0:T(8,128)(2,1)}, f32[768,128]{1,0:T(8,128)}, bf16[384,3072]{1,0:T(8,128)(2,1)}, bf16[384,3072]{1,0:T(8,128)(2,1)}) custom-call(s32[2]{0:T(128)} %pad_add_fusion.info.refs_0_, bf16[1024,768]{1,0:T(8,128)(2,1)} %get-tuple-element.130.refs_1_, ...), custom_call_target="tpu_custom_call" | custom-call | flops 14000000000 | bytes 42000000 | tf_op jit(solution)/shard_map/feed_forward/pallas_call | solution.py:409
  159.7 4.7 %collective-permute-start.7 = (bf16[96,1792]{1,0:T(8,128)(2,1)S(1)}, bf16[96,1792]{1,0:T(8,128)(2,1)S(1)}, u32[]{:S(2)}, u32[]{:S(2)}) collective-permute-start(bf16[96,1792]{1,0:T(8,128)(2,1)S(1)} %bitcast.211), channel_id=1, source_target_pairs={{0,4},{1,5},{2,6},{3,7},{4,0},{5,1},{6,2},{7,3},{8,12},{9,13},{10,... | collective-permute-start | bytes 1032200 | tf_op jit(solution)/shard_map/ppermute | solution.py:505
  164.4 18.4 %feed_forward.3 = (bf16[1024,1536]{1,0:T(8,128)(2,1)}, bf16[1024,1536]{1,0:T(8,128)(2,1)}, bf16[384,3200]{1,0:T(8,128)(2,1)}, bf16[384,3200]{1,0:T(8,128)(2,1)}) custom-call(s32[2]{0:T(128)} %pad_add_fusion.info.refs_0_, bf16[1024,768]{1,0:T(8,128)(2,1)} %get-tuple-element.130.refs_1_, bf16[1024,768]{1,0:T(8,128)(2,1)} %get-tuple-element.131.gy_ref.refs_2_, ...), custom_call_target="tpu_custom_call" | custom-call | flops 14000000000 | bytes 42000000 | tf_op jit(solution)/shard_map/feed_forward/pallas_call | solution.py:409
  182.9 2.6 add_convert_fusion.1
  190.0 1.8 collective-permute-start.11
  192.0 12.5 %layer_output.1 = bf16[1024,768]{1,0:T(8,128)(2,1)} custom-call(s32[2]{0:T(128)} %pad_add_fusion.info.refs_0_, bf16[1024,768]{1,0:T(8,128)(2,1)} %bitcast.236, bf16[1024,768]{1,0:T(8,128)(2,1)} %get-tuple-element.104.mix_ref.refs_2_, bf16[768,1792]{1,0:T(8,128)(2,1)} %bitcast.195, bf16[768,6144]{1,0:T(8,128)(2,1)} %all-gather.2.cloned.1.call-done.refs_3_.refs_4_.refs_5_, ...), custom_call_target="tpu_custom_call" | custom-call | flops 8999999488 | bytes 27000000 | tf_op jit(solution)/shard_map/layer_output/pallas_call | solution.py:448
  204.5 3.1 %collective-permute-done.12 = bf16[48,1792]{1,0:T(8,128)(2,1)S(1)} collective-permute-done((bf16[48,1792]{1,0:T(8,128)(2,1)}, bf16[48,1792]{1,0:T(8,128)(2,1)S(1)}, u32[]{:S(2)}, u32[]{:S(2)}) %collective-permute-start.12) | collective-permute-done | bytes 172064 | tf_op jit(solution)/shard_map/ppermute | solution.py:505
  211.7 2.4 add_convert_fusion
  218.3 1.8 collective-permute-start.14
  222.4 14.1 %token_grads.1 = f32[1024,768]{1,0:T(8,128)} custom-call(bf16[1024,768]{1,0:T(8,128)(2,1)} %bitcast.237, bf16[1024,768]{1,0:T(8,128)(2,1)} %bitcast.239, bf16[1024,768]{1,0:T(8,128)(2,1)} %get-tuple-element.105.dq_ref.refs_2_, bf16[1024,128]{1,0:T(8,128)(2,1)} %get-tuple-element.106.dkv_ref.refs_3_, bf16[768,1792]{1,0:T(8,128)(2,1)} %bitcast.196, ...), custom_call_target="tpu_custom_call" | custom-call | flops 11000000512 | bytes 33000000 | tf_op jit(solution)/shard_map/token_grads/pallas_call | solution.py:486
  236.5 4.4 %collective-permute-done.17 = bf16[24,1792]{1,0:T(8,128)(2,1)S(1)} collective-permute-done((bf16[24,1792]{1,0:T(8,128)(2,1)S(1)}, bf16[24,1792]{1,0:T(8,128)(2,1)S(1)}, u32[]{:S(2)}, u32[]{:S(2)}) %collective-permute-start.17) | collective-permute-done | bytes 86048 | tf_op jit(solution)/shard_map/ppermute | solution.py:505
  246.5 1.8 collective-permute-start.20
  249.0 3.1 %collective-permute-done.18 = bf16[48,3072]{1,0:T(8,128)(2,1)S(1)} collective-permute-done((bf16[48,3072]{1,0:T(8,128)(2,1)S(1)}, bf16[48,3072]{1,0:T(8,128)(2,1)S(1)}, u32[]{:S(2)}, u32[]{:S(2)}) %collective-permute-start.18) | collective-permute-done | bytes 294944 | tf_op jit(solution)/shard_map/ppermute | solution.py:505
  252.2 1.8 collective-permute-done.20
  254.3 1.7 collective-permute-start.22
  258.7 4.7 %collective-permute-done.21 = bf16[24,3072]{1,0:T(8,128)(2,1)S(1)} collective-permute-done((bf16[24,3072]{1,0:T(8,128)(2,1)S(1)}, bf16[24,3072]{1,0:T(8,128)(2,1)S(1)}, u32[]{:S(2)}, u32[]{:S(2)}) %collective-permute-start.21) | collective-permute-done | bytes 147488 | tf_op jit(solution)/shard_map/ppermute | solution.py:505
  264.0 3.1 %collective-permute-start.23 = (bf16[24,3200]{1,0:T(8,128)(2,1)S(1)}, bf16[24,3200]{1,0:T(8,128)(2,1)S(1)}, u32[]{:S(2)}, u32[]{:S(2)}) collective-permute-start(bf16[24,3200]{1,0:T(8,128)(2,1)S(1)} %dynamic-slice_bitcast_fusion), channel_id=1, source_target_pairs={{0,4},{1,5},{2,6},{3,7},{4,0},{5,1},{6,2},{7,3},{8,12},{9,13},{10,... | collective-permute-start | bytes 460808 | tf_op jit(solution)/shard_map/ppermute | solution.py:505
  267.2 4.7 %collective-permute-done.23 = bf16[24,3200]{1,0:T(8,128)(2,1)S(1)} collective-permute-done((bf16[24,3200]{1,0:T(8,128)(2,1)S(1)}, bf16[24,3200]{1,0:T(8,128)(2,1)S(1)}, u32[]{:S(2)}, u32[]{:S(2)}) %collective-permute-start.23) | collective-permute-done | bytes 153632 | tf_op jit(solution)/shard_map/ppermute | solution.py:505
  276.0 2.6 reshape.1435
  (157 shorter events, 45.0 us)
Async XLA Ops:
  7.2 134.5 %all-gather.2.cloned.1.call-start = ((), (), s32[]{:S(2)}) async-start(), calls=%async_computation | async-start | bytes 9732096 | tf_op jit(solution)/shard_map/all_gather | solution.py:617
  10.5 3.1 %copy-start.9 = (bf16[24,768]{1,0:T(8,128)(2,1)S(1)}, bf16[24,768]{1,0:T(8,128)(2,1)}, u32[]{:S(2)}) copy-start(bf16[24,768]{1,0:T(8,128)(2,1)} %param.25) | copy-start | bytes 110596
  10.5 3.1 %copy-start.10 = (bf16[24,768]{1,0:T(8,128)(2,1)S(1)}, bf16[24,768]{1,0:T(8,128)(2,1)}, u32[]{:S(2)}) copy-start(bf16[24,768]{1,0:T(8,128)(2,1)} %param.21) | copy-start | bytes 110596
  10.5 3.1 %copy-start.11 = (bf16[24,128]{1,0:T(8,128)(2,1)S(1)}, bf16[24,128]{1,0:T(8,128)(2,1)}, u32[]{:S(2)}) copy-start(bf16[24,128]{1,0:T(8,128)(2,1)} %param.23) | copy-start | bytes 18436
  13.6 8.5 %collective-permute-start = (bf16[24,1792]{1,0:T(8,128)(2,1)S(1)}, bf16[24,1792]{1,0:T(8,128)(2,1)S(1)}, u32[]{:S(2)}, u32[]{:S(2)}) collective-permute-start(bf16[24,1792]{1,0:T(8,128)(2,1)S(1)} %pad_maximum_fusion.12), channel_id=1, source_target_pairs={{0,4},{1,5},{2,6},{3,7},{4,0},{5,1},{6,2},{7,3},{8,12},{9,13},{10,... | collective-permute-start | bytes 258056 | tf_op jit(solution)/shard_map/ppermute | solution.py:505
  22.2 7.6 %collective-permute-start.1 = (bf16[48,1792]{1,0:T(8,128)(2,1)S(1)}, bf16[48,1792]{1,0:T(8,128)(2,1)S(1)}, u32[]{:S(2)}, u32[]{:S(2)}) collective-permute-start(bf16[48,1792]{1,0:T(8,128)(2,1)S(1)} %bitcast.226), channel_id=1, source_target_pairs={{0,2},{1,3},{2,0},{3,1},{4,6},{5,7},{6,4},{7,5},{8,10},{9,11},{10,... | collective-permute-start | bytes 516104 | tf_op jit(solution)/shard_map/ppermute | solution.py:505
  29.8 7.3 %collective-permute-start.2 = (bf16[96,1792]{1,0:T(8,128)(2,1)S(1)}, bf16[96,1792]{1,0:T(8,128)(2,1)S(1)}, u32[]{:S(2)}, u32[]{:S(2)}) collective-permute-start(bf16[96,1792]{1,0:T(8,128)(2,1)S(1)} %bitcast.212), channel_id=1, source_target_pairs={{0,16},{8,24},{16,0},{24,8},{1,17},{9,25},{17,1},{25,9},{2,18},{10... | collective-permute-start | bytes 1032200 | tf_op jit(solution)/shard_map/ppermute | solution.py:505
  37.3 21.9 %collective-permute-start.3 = (bf16[192,1792]{1,0:T(8,128)(2,1)S(1)}, bf16[192,1792]{1,0:T(8,128)(2,1)S(1)}, u32[]{:S(2)}, u32[]{:S(2)}) collective-permute-start(bf16[192,1792]{1,0:T(8,128)(2,1)S(1)} %bitcast.203), channel_id=1, source_target_pairs={{0,1},{1,0},{2,3},{3,2},{4,5},{5,4},{6,7},{7,6},{8,9},{9,8},{10,11... | collective-permute-start | bytes 2064392 | tf_op jit(solution)/shard_map/ppermute | solution.py:505
  60.7 3.3 %collective-permute-start.4 = (bf16[384,1792]{1,0:T(8,128)(2,1)}, bf16[384,1792]{1,0:T(8,128)(2,1)S(1)}, u32[]{:S(2)}, u32[]{:S(2)}) collective-permute-start(bf16[384,1792]{1,0:T(8,128)(2,1)} %bitcast.42), channel_id=1, source_target_pairs={{0,8},{8,0},{16,24},{24,16},{1,9},{9,1},{17,25},{25,17},{2,10},{10... | collective-permute-start | bytes 4128776 | tf_op jit(solution)/shard_map/ppermute | solution.py:505
  133.6 3.3 %collective-permute-start.5 = (bf16[384,1792]{1,0:T(8,128)(2,1)}, bf16[384,1792]{1,0:T(8,128)(2,1)S(1)}, u32[]{:S(2)}, u32[]{:S(2)}) collective-permute-start(bf16[384,1792]{1,0:T(8,128)(2,1)} %get-tuple-element.110), channel_id=1, source_target_pairs={{0,8},{8,0},{16,24},{24,16},{1,9},{9,1},{17,25},{25,17},{2,10},{10... | collective-permute-start | bytes 4128776 | tf_op jit(solution)/shard_map/ppermute | solution.py:505
  138.6 20.8 %collective-permute-start.6 = (bf16[192,1792]{1,0:T(8,128)(2,1)S(1)}, bf16[192,1792]{1,0:T(8,128)(2,1)S(1)}, u32[]{:S(2)}, u32[]{:S(2)}) collective-permute-start(bf16[192,1792]{1,0:T(8,128)(2,1)S(1)} %bitcast.205), channel_id=1, source_target_pairs={{0,2},{1,3},{2,0},{3,1},{4,6},{5,7},{6,4},{7,5},{8,10},{9,11},{10,... | collective-permute-start | bytes 2064392 | tf_op jit(solution)/shard_map/ppermute | solution.py:505
  159.6 23.2 %collective-permute-start.8 = (bf16[384,3072]{1,0:T(8,128)(2,1)}, bf16[384,3072]{1,0:T(8,128)(2,1)}, u32[]{:S(2)}, u32[]{:S(2)}) collective-permute-start(bf16[384,3072]{1,0:T(8,128)(2,1)} %get-tuple-element.129), channel_id=1, source_target_pairs={{0,8},{8,0},{16,24},{24,16},{1,9},{9,1},{17,25},{25,17},{2,10},{10... | collective-permute-start | bytes 7077896 | tf_op jit(solution)/shard_map/ppermute | solution.py:505
  159.7 23.1 %collective-permute-start.7 = (bf16[96,1792]{1,0:T(8,128)(2,1)S(1)}, bf16[96,1792]{1,0:T(8,128)(2,1)S(1)}, u32[]{:S(2)}, u32[]{:S(2)}) collective-permute-start(bf16[96,1792]{1,0:T(8,128)(2,1)S(1)} %bitcast.211), channel_id=1, source_target_pairs={{0,4},{1,5},{2,6},{3,7},{4,0},{5,1},{6,2},{7,3},{8,12},{9,13},{10,... | collective-permute-start | bytes 1032200 | tf_op jit(solution)/shard_map/ppermute | solution.py:505
  164.4 18.5 %copy-start.1 = (bf16[384,3072]{1,0:T(8,128)(2,1)S(1)}, bf16[384,3072]{1,0:T(8,128)(2,1)}, u32[]{:S(2)}) copy-start(bf16[384,3072]{1,0:T(8,128)(2,1)} %get-tuple-element.138) | copy-start | bytes 7077892
  188.1 19.5 %collective-permute-start.9 = (bf16[384,3200]{1,0:T(8,128)(2,1)}, bf16[384,3200]{1,0:T(8,128)(2,1)}, u32[]{:S(2)}, u32[]{:S(2)}) collective-permute-start(bf16[384,3200]{1,0:T(8,128)(2,1)} %get-tuple-element.143), channel_id=1, source_target_pairs={{0,8},{8,0},{16,24},{24,16},{1,9},{9,1},{17,25},{25,17},{2,10},{10... | collective-permute-start | bytes 7372808 | tf_op jit(solution)/shard_map/ppermute | solution.py:505
  188.5 19.1 %collective-permute-start.10 = (bf16[192,1536]{1,0:T(8,128)(2,1)S(1)}, bf16[192,1536]{1,0:T(8,128)(2,1)}, u32[]{:S(2)}, u32[]{:S(2)}) collective-permute-start(bf16[192,1536]{1,0:T(8,128)(2,1)S(1)} %bitcast.206), channel_id=1, source_target_pairs={{0,1},{1,0},{2,3},{3,2},{4,5},{5,4},{6,7},{7,6},{8,9},{9,8},{10,11... | collective-permute-start | bytes 1769480 | tf_op jit(solution)/shard_map/ppermute | solution.py:505
  190.0 17.7 %collective-permute-start.11 = (bf16[192,1536]{1,0:T(8,128)(2,1)S(1)}, bf16[192,1536]{1,0:T(8,128)(2,1)}, u32[]{:S(2)}, u32[]{:S(2)}) collective-permute-start(bf16[192,1536]{1,0:T(8,128)(2,1)S(1)} %bitcast.207), channel_id=1, source_target_pairs={{0,16},{8,24},{16,0},{24,8},{1,17},{9,25},{17,1},{25,9},{2,18},{10... | collective-permute-start | bytes 1769480 | tf_op jit(solution)/shard_map/ppermute | solution.py:505
  191.7 15.9 %collective-permute-start.12 = (bf16[48,1792]{1,0:T(8,128)(2,1)}, bf16[48,1792]{1,0:T(8,128)(2,1)S(1)}, u32[]{:S(2)}, u32[]{:S(2)}) collective-permute-start(bf16[48,1792]{1,0:T(8,128)(2,1)} %bitcast.225), channel_id=1, source_target_pairs={{0,1},{1,0},{2,3},{3,2},{4,5},{5,4},{6,7},{7,6},{8,9},{9,8},{10,11... | collective-permute-start | bytes 516104 | tf_op jit(solution)/shard_map/ppermute | solution.py:505
  207.6 3.4 %copy-start.7 = (bf16[48,1792]{1,0:T(8,128)(2,1)}, bf16[48,1792]{1,0:T(8,128)(2,1)S(1)}, u32[]{:S(2)}) copy-start(bf16[48,1792]{1,0:T(8,128)(2,1)S(1)} %collective-permute-done.12) | copy-start | bytes 516100
  216.9 24.0 %collective-permute-start.13 = (bf16[96,1536]{1,0:T(8,128)(2,1)}, bf16[96,1536]{1,0:T(8,128)(2,1)S(1)}, u32[]{:S(2)}, u32[]{:S(2)}) collective-permute-start(bf16[96,1536]{1,0:T(8,128)(2,1)} %bitcast.62), channel_id=1, source_target_pairs={{0,16},{8,24},{16,0},{24,8},{1,17},{9,25},{17,1},{25,9},{2,18},{10... | collective-permute-start | bytes 884744 | tf_op jit(solution)/shard_map/ppermute | solution.py:505
  218.3 22.5 %collective-permute-start.14 = (bf16[96,1536]{1,0:T(8,128)(2,1)}, bf16[96,1536]{1,0:T(8,128)(2,1)}, u32[]{:S(2)}, u32[]{:S(2)}) collective-permute-start(bf16[96,1536]{1,0:T(8,128)(2,1)} %bitcast.64), channel_id=1, source_target_pairs={{0,1},{1,0},{2,3},{3,2},{4,5},{5,4},{6,7},{7,6},{8,9},{9,8},{10,11... | collective-permute-start | bytes 884744 | tf_op jit(solution)/shard_map/ppermute | solution.py:505
  220.1 20.8 %collective-permute-start.15 = (bf16[192,1536]{1,0:T(8,128)(2,1)}, bf16[192,1536]{1,0:T(8,128)(2,1)}, u32[]{:S(2)}, u32[]{:S(2)}) collective-permute-start(bf16[192,1536]{1,0:T(8,128)(2,1)} %bitcast.66), channel_id=1, source_target_pairs={{0,1},{1,0},{2,3},{3,2},{4,5},{5,4},{6,7},{7,6},{8,9},{9,8},{10,11... | collective-permute-start | bytes 1769480 | tf_op jit(solution)/shard_map/ppermute | solution.py:505
  220.4 20.5 %collective-permute-start.16 = (bf16[192,1664]{1,0:T(8,128)(2,1)}, bf16[192,1664]{1,0:T(8,128)(2,1)}, u32[]{:S(2)}, u32[]{:S(2)}) collective-permute-start(bf16[192,1664]{1,0:T(8,128)(2,1)} %bitcast.68), channel_id=1, source_target_pairs={{0,16},{8,24},{16,0},{24,8},{1,17},{9,25},{17,1},{25,9},{2,18},{10... | collective-permute-start | bytes 1916936 | tf_op jit(solution)/shard_map/ppermute | solution.py:505
  220.9 19.9 %collective-permute-start.17 = (bf16[24,1792]{1,0:T(8,128)(2,1)S(1)}, bf16[24,1792]{1,0:T(8,128)(2,1)S(1)}, u32[]{:S(2)}, u32[]{:S(2)}) collective-permute-start(bf16[24,1792]{1,0:T(8,128)(2,1)S(1)} %dynamic-slice_bitcast_fusion.2), channel_id=1, source_target_pairs={{0,16},{8,24},{16,0},{24,8},{1,17},{9,25},{17,1},{25,9},{2,18},{10... | collective-permute-start | bytes 258056 | tf_op jit(solution)/shard_map/ppermute | solution.py:505
  243.4 4.9 %copy-start.5 = (bf16[2,1,1,1,1,24,1792]{6,5,4,3,2,1,0:T(8,128)(2,1)S(1)}, bf16[2,1,1,1,1,24,1792]{6,5,4,3,2,1,0:T(8,128)(2,1)}, u32[]{:S(2)}) copy-start(bf16[2,1,1,1,1,24,1792]{6,5,4,3,2,1,0:T(8,128)(2,1)} %copy-done.4) | copy-start | bytes 516100
  244.6 7.5 %collective-permute-start.18 = (bf16[48,3072]{1,0:T(8,128)(2,1)S(1)}, bf16[48,3072]{1,0:T(8,128)(2,1)S(1)}, u32[]{:S(2)}, u32[]{:S(2)}) collective-permute-start(bf16[48,3072]{1,0:T(8,128)(2,1)S(1)} %bitcast.218), channel_id=1, source_target_pairs={{0,2},{1,3},{2,0},{3,1},{4,6},{5,7},{6,4},{7,5},{8,10},{9,11},{10,... | collective-permute-start | bytes 884744 | tf_op jit(solution)/shard_map/ppermute | solution.py:505
  244.9 7.3 %collective-permute-start.19 = (bf16[96,1536]{1,0:T(8,128)(2,1)S(1)}, bf16[96,1536]{1,0:T(8,128)(2,1)S(1)}, u32[]{:S(2)}, u32[]{:S(2)}) collective-permute-start(bf16[96,1536]{1,0:T(8,128)(2,1)S(1)} %bitcast.220), channel_id=1, source_target_pairs={{0,16},{8,24},{16,0},{24,8},{1,17},{9,25},{17,1},{25,9},{2,18},{10... | collective-permute-start | bytes 884744 | tf_op jit(solution)/shard_map/ppermute | solution.py:505
  246.5 7.5 %collective-permute-start.20 = (bf16[96,1664]{1,0:T(8,128)(2,1)S(1)}, bf16[96,1664]{1,0:T(8,128)(2,1)S(1)}, u32[]{:S(2)}, u32[]{:S(2)}) collective-permute-start(bf16[96,1664]{1,0:T(8,128)(2,1)S(1)} %bitcast.214), channel_id=1, source_target_pairs={{0,1},{1,0},{2,3},{3,2},{4,5},{5,4},{6,7},{7,6},{8,9},{9,8},{10,11... | collective-permute-start | bytes 958472 | tf_op jit(solution)/shard_map/ppermute | solution.py:505
  254.3 9.6 %collective-permute-start.22 = (bf16[48,3200]{1,0:T(8,128)(2,1)S(1)}, bf16[48,3200]{1,0:T(8,128)(2,1)S(1)}, u32[]{:S(2)}, u32[]{:S(2)}) collective-permute-start(bf16[48,3200]{1,0:T(8,128)(2,1)S(1)} %bitcast.215), channel_id=1, source_target_pairs={{0,2},{1,3},{2,0},{3,1},{4,6},{5,7},{6,4},{7,5},{8,10},{9,11},{10,... | collective-permute-start | bytes 921608 | tf_op jit(solution)/shard_map/ppermute | solution.py:505
  256.7 6.7 %collective-permute-start.21 = (bf16[24,3072]{1,0:T(8,128)(2,1)S(1)}, bf16[24,3072]{1,0:T(8,128)(2,1)S(1)}, u32[]{:S(2)}, u32[]{:S(2)}) collective-permute-start(bf16[24,3072]{1,0:T(8,128)(2,1)S(1)} %dynamic-slice_bitcast_fusion.1), channel_id=1, source_target_pairs={{0,4},{1,5},{2,6},{3,7},{4,0},{5,1},{6,2},{7,3},{8,12},{9,13},{10,... | collective-permute-start | bytes 442376 | tf_op jit(solution)/shard_map/ppermute | solution.py:505
  258.0 22.1 %copy-start.12 = (f32[24]{0:T(128)}, f32[24]{0:T(128)S(1)}, u32[]{:S(2)}) copy-start(f32[24]{0:T(128)S(1)} %get-tuple-element.249) | copy-start | bytes 292
  264.0 7.9 %collective-permute-start.23 = (bf16[24,3200]{1,0:T(8,128)(2,1)S(1)}, bf16[24,3200]{1,0:T(8,128)(2,1)S(1)}, u32[]{:S(2)}, u32[]{:S(2)}) collective-permute-start(bf16[24,3200]{1,0:T(8,128)(2,1)S(1)} %dynamic-slice_bitcast_fusion), channel_id=1, source_target_pairs={{0,4},{1,5},{2,6},{3,7},{4,0},{5,1},{6,2},{7,3},{8,12},{9,13},{10,... | collective-permute-start | bytes 460808 | tf_op jit(solution)/shard_map/ppermute | solution.py:505
  (15 other events, 28.9 us)
Sparse Core Ops, SparseCore 0:
  12.8 92.9 all-gather.1
